TPU v7x, 256 devices: a whole 4x4x8 slice. The times are simulated.
256 devices in a mesh: region: 8 (over x, core), box: 32 (over y, z).
Axes of the slice: x: 4, y: 4, z: 8, core: 2. Of those that a mesh axis runs over, the one named last changes fastest.
Arguments:
- kept_diagonal_tile: bfloat16 [512, 512, 512], P(('region', 'box')), may hold values from -6 to 6
- discard_reciprocal: bfloat16 [512, 512, 512], P(('region', 'box')), may hold values from -0.25 to 0.25
- discard_by_kept: bfloat16 [512, 512, 512], P(('region', 'box')), may hold values from -6 to 6
- kept_by_discard: bfloat16 [512, 512, 512], P(('region', 'box')), may hold values from -0.25 to 0.25
- adjacent_discard_to_kept: bfloat16 [512, 4, 512, 512], P(('region', 'box')), may hold values from -0.25 to 0.25
- adjacent_kept_to_discard: bfloat16 [512, 4, 512, 512], P(('region', 'box')), may hold values from -6 to 6
- adjacent_site_table: int32 [512, 4], P(('region', 'box')), may hold values from 0 to 2
- retained_slots: int32 [512, 256], P(('region', 'box')), may hold values from 0 to 511, as said below
- kept_list_length: int32 [512], P(('region', 'box')), may hold values from 128 to 256, as said below
- ancestor_site_map: int32 [512], P(('region', 'box')), may hold values from 0 to 15, as said below
Outputs:
- parent_blocks: bfloat16 [512, 256, 256], P(('region', 'box'))
Inputs may be any that keep to these rules, and one draw needn't show every extreme that they name: `retained_slots`: each row holds 256 different tile positions. `kept_list_length`: some box has all 256 entries valid. `ancestor_site_map`: among the boxes of one position j, every value from 0 to 15 occurs exactly once. `adjacent_site_table`: the value 2 marks an absent neighbour.
All inputs are finite; a program needn't handle non-finite values.
Results may differ from a plain program's by a relative error of at most 0.0053.
Values may be sent and summed in bfloat16 or wider, within the bound.
No kernel may reach another device: no remote copies, remote signals or barrier semaphores. Data moves between devices by JAX's collectives and lax.ppermute only.
A program may use at most 128 MiB of HBM per device.

v0:
```python
import jax
import jax.numpy as jnp
from jax import lax
from jax.sharding import PartitionSpec as P

offsets_list = (1, -1, 2, -2)


def from_behind(value, axis, by):
    length = lax.axis_size(axis)
    pairs = [(i, i + by) for i in range(length) if 0 <= i + by < length]
    return lax.ppermute(value, axis, pairs)


def local(
    kept_diagonal_tile,
    discard_reciprocal,
    discard_by_kept,
    kept_by_discard,
    adjacent_discard_to_kept,
    adjacent_kept_to_discard,
    adjacent_site_table,
    retained_slots,
    kept_list_length,
    ancestor_site_map,
):
    places = kept_diagonal_tile.shape[0]
    tile_span = retained_slots.shape[1]
    regions = lax.axis_size("region")
    solution_block = jnp.einsum(
        "mjq,mqc->mjc", discard_reciprocal, discard_by_kept, preferred_element_type=jnp.float32
    ).astype(jnp.bfloat16)
    self_update = jnp.einsum(
        "lsa,lat->lst", kept_by_discard, solution_block, preferred_element_type=jnp.float32
    )
    reduced = jnp.einsum(
        "lab,lkbs->lkas",
        discard_reciprocal,
        adjacent_kept_to_discard,
        preferred_element_type=jnp.float32,
    ).astype(jnp.bfloat16)
    near_update = jnp.einsum(
        "lksa,lkat->lkst", adjacent_discard_to_kept, reduced, preferred_element_type=jnp.float32
    )
    hits = adjacent_site_table[:, :, None] == jnp.arange(places, dtype=jnp.int32)[None, None, :]
    outgoing = jnp.sum(
        jnp.where(hits[:, :, :, None, None], near_update[:, :, None], jnp.float32(0.0)), axis=0
    ).astype(jnp.bfloat16)
    refreshed_submatrix = kept_diagonal_tile.astype(jnp.float32) - self_update
    for which, offset in enumerate(offsets_list):
        refreshed_submatrix = refreshed_submatrix - from_behind(
            outgoing[which], "box", offset
        ).astype(jnp.float32)
    picked_values = jax.vmap(
        lambda dense_submatrix, element_slot: dense_submatrix[element_slot][:, element_slot]
    )(refreshed_submatrix, retained_slots)
    valid = jnp.arange(tile_span, dtype=jnp.int32)[None, :] < kept_list_length[:, None]
    child = jnp.where(
        valid[:, :, None] & valid[:, None, :], picked_values, jnp.float32(0.0)
    ).astype(jnp.bfloat16)
    owners = ancestor_site_map[None, :] == jnp.arange(regions * places, dtype=jnp.int32)[:, None]
    placed = jnp.sum(
        jnp.where(owners[:, :, None, None], child.astype(jnp.float32)[None], jnp.float32(0.0)),
        axis=1,
    )
    result = lax.psum_scatter(
        placed.astype(jnp.bfloat16), "region", scatter_dimension=0, tiled=True
    )
    return result


def solution(mesh):
    in_specs = (
        P(("region", "box"), None, None),
        P(("region", "box"), None, None),
        P(("region", "box"), None, None),
        P(("region", "box"), None, None),
        P(("region", "box"), None, None, None),
        P(("region", "box"), None, None, None),
        P(("region", "box"), None),
        P(("region", "box"), None),
        P(("region", "box")),
        P(("region", "box")),
    )
    out_specs = P(("region", "box"), None, None)
    return jax.shard_map(local, mesh=mesh, in_specs=in_specs, out_specs=out_specs, check_vma=False)
```

profile of v0, /device:TPU:25, one launch (start us, length us, event | category | flops | bytes accessed | tf_op | source)
XLA Modules:
  0.0 184.9 jit_solution(10716234726736954001)
XLA Ops:
  6.5 0.0 copy-start
  6.5 0.0 reduce-scatter.2.cloned.1.call-start
  6.5 1.2 copy-done
  7.8 11.2 %fusion.2 = f32[2,4,512,512]{2,3,1,0:T(8,128)} fusion(bf16[2,4,512,512]{3,2,1,0:T(8,128)(2,1)} %param.14, bf16[2,4,512,512]{3,2,1,0:T(8,128)(2,1)} %param.15, bf16[2,512,512]{2,1,0:T(8,128)(2,1)S(1)} %copy-done), kind=kOutput, calls=%fused_computation.6 | convolution fusion | flops 4297064448 | bytes 17825792 | tf_op jit(solution)/shard_map/lksa,lkat->lkst/dot_general | solution.py:42
  19.0 9.9 %copy.17 = f32[2,4,512,512]{3,2,1,0:T(8,128)} copy(f32[2,4,512,512]{2,3,1,0:T(8,128)} %fusion.2) | data formatting | bytes 16777216 | tf_op jit(solution)/shard_map/lksa,lkat->lkst/dot_general | solution.py:42
  28.9 0.0 copy-done.3
  28.9 0.1 iota_compare_fusion.1
  29.0 8.4 %select_reduce_fusion = bf16[4,2,512,512]{3,2,1,0:T(8,128)(2,1)} fusion(f32[2,4,512,512]{3,2,1,0:T(8,128)} %copy.17, pred[2,4,2]{2,1,0:T(4,128)(4,1)S(1)} %iota_compare_fusion.1), kind=kLoop, calls=%fused_computation.2 | loop fusion | flops 6291456 | bytes 12582928 | tf_op jit(solution)/shard_map/reduce_sum | solution.py:46
  37.4 7.3 %copy.18 = bf16[4,2,512,512]{2,3,1,0:T(8,128)(2,1)} copy(bf16[4,2,512,512]{3,2,1,0:T(8,128)(2,1)} %select_reduce_fusion) | data formatting | bytes 8388608 | tf_op jit(solution)/shard_map/reduce_sum | solution.py:46
  44.7 4.4 %slice_bitcast_fusion.3 = (bf16[2,512,512]{1,2,0:T(8,128)(2,1)}, bf16[2,512,512]{1,2,0:T(8,128)(2,1)}, bf16[2,512,512]{1,2,0:T(8,128)(2,1)}, bf16[2,512,512]{1,2,0:T(8,128)(2,1)}) fusion(bf16[4,2,512,512]{2,3,1,0:T(8,128)(2,1)} %copy.18), kind=kLoop, calls=%fused_computation.17 | loop fusion | bytes 8388608 | tf_op jit(solution)/shard_map/squeeze | solution.py:52
  49.1 3.5 %collective-permute-start = (bf16[2,512,512]{1,2,0:T(8,128)(2,1)}, bf16[2,512,512]{1,2,0:T(8,128)(2,1)}, u32[]{:S(2)}, u32[]{:S(2)}) collective-permute-start(bf16[2,512,512]{1,2,0:T(8,128)(2,1)} %get-tuple-element.5), channel_id=1, source_target_pairs={{0,1},{1,2},{2,3},{3,4},{4,5},{5,6},{6,7},{7,8},{8,9},{9,10},{10,1... | collective-permute-start | bytes 3145736 | tf_op jit(solution)/shard_map/ppermute | solution.py:12
  52.6 6.0 %collective-permute-start.1 = (bf16[2,512,512]{1,2,0:T(8,128)(2,1)}, bf16[2,512,512]{1,2,0:T(8,128)(2,1)}, u32[]{:S(2)}, u32[]{:S(2)}) collective-permute-start(bf16[2,512,512]{1,2,0:T(8,128)(2,1)} %get-tuple-element.7), channel_id=1, source_target_pairs={{1,0},{2,1},{3,2},{4,3},{5,4},{6,5},{7,6},{8,7},{9,8},{10,9},{11,1... | collective-permute-start | bytes 3145736 | tf_op jit(solution)/shard_map/ppermute | solution.py:12
  58.7 1.9 %collective-permute-start.2 = (bf16[2,512,512]{1,2,0:T(8,128)(2,1)}, bf16[2,512,512]{1,2,0:T(8,128)(2,1)}, u32[]{:S(2)}, u32[]{:S(2)}) collective-permute-start(bf16[2,512,512]{1,2,0:T(8,128)(2,1)} %get-tuple-element.6), channel_id=1, source_target_pairs={{0,2},{1,3},{2,4},{3,5},{4,6},{5,7},{6,8},{7,9},{8,10},{9,11},{10,... | collective-permute-start | bytes 3145736 | tf_op jit(solution)/shard_map/ppermute | solution.py:12
  60.6 6.6 %collective-permute-start.3 = (bf16[2,512,512]{1,2,0:T(8,128)(2,1)}, bf16[2,512,512]{1,2,0:T(8,128)(2,1)}, u32[]{:S(2)}, u32[]{:S(2)}) collective-permute-start(bf16[2,512,512]{1,2,0:T(8,128)(2,1)} %get-tuple-element.8), channel_id=1, source_target_pairs={{2,0},{3,1},{4,2},{5,3},{6,4},{7,5},{8,6},{9,7},{10,8},{11,9},{12,... | collective-permute-start | bytes 3145736 | tf_op jit(solution)/shard_map/ppermute | solution.py:12
  67.2 0.0 copy-done.1
  67.2 0.5 copy.16
  67.8 0.1 iota_compare_fusion.2
  67.8 0.0 copy-done.4
  67.8 12.1 %collective-permute-done = bf16[2,512,512]{1,2,0:T(8,128)(2,1)} collective-permute-done((bf16[2,512,512]{1,2,0:T(8,128)(2,1)}, bf16[2,512,512]{1,2,0:T(8,128)(2,1)}, u32[]{:S(2)}, u32[]{:S(2)}) %collective-permute-start) | collective-permute-done | bytes 1048608 | tf_op jit(solution)/shard_map/ppermute | solution.py:12
  79.9 2.1 %collective-permute-done.1 = bf16[2,512,512]{1,2,0:T(8,128)(2,1)} collective-permute-done((bf16[2,512,512]{1,2,0:T(8,128)(2,1)}, bf16[2,512,512]{1,2,0:T(8,128)(2,1)}, u32[]{:S(2)}, u32[]{:S(2)}) %collective-permute-start.1) | collective-permute-done | bytes 1048608 | tf_op jit(solution)/shard_map/ppermute | solution.py:12
  82.0 22.5 %collective-permute-done.2 = bf16[2,512,512]{1,2,0:T(8,128)(2,1)} collective-permute-done((bf16[2,512,512]{1,2,0:T(8,128)(2,1)}, bf16[2,512,512]{1,2,0:T(8,128)(2,1)}, u32[]{:S(2)}, u32[]{:S(2)}) %collective-permute-start.2) | collective-permute-done | bytes 1048608 | tf_op jit(solution)/shard_map/ppermute | solution.py:12
  104.5 21.3 %collective-permute-done.3 = bf16[2,512,512]{1,2,0:T(8,128)(2,1)} collective-permute-done((bf16[2,512,512]{1,2,0:T(8,128)(2,1)}, bf16[2,512,512]{1,2,0:T(8,128)(2,1)}, u32[]{:S(2)}, u32[]{:S(2)}) %collective-permute-start.3) | collective-permute-done | bytes 1048608 | tf_op jit(solution)/shard_map/ppermute | solution.py:12
  125.7 5.5 %fusion.10 = bf16[2,512,512]{1,2,0:T(8,128)(2,1)} fusion(bf16[2,512,512]{1,2,0:T(8,128)(2,1)} %collective-permute-done.3, bf16[2,512,512]{1,2,0:T(8,128)(2,1)} %collective-permute-done.2, bf16[2,512,512]{1,2,0:T(8,128)(2,1)} %collective-permute-done.1, bf16[2,512,512]{1,2,0:T(8,128)(2,1)} %collective-permute-done, bf16[2,512,512]{1,2,0:T(8,128)(2,1)S(1)} %copy.16, ...), kind=kOutput, calls=%fused_computation.12 | convolution fusion | flops 1080033280 | bytes 9437184 | tf_op jit(solution)/shard_map/lsa,lat->lst/dot_general | solution.py:33
  131.2 1.5 copy.19
  132.7 3.9 %gather_fusion = bf16[512,512]{1,0:T(8,128)(2,1)S(1)} fusion(bf16[2,512,512]{2,1,0:T(8,128)(2,1)S(1)} %copy.19, s32[512]{0:T(512)S(1)} %bitcast.45), kind=kCustom, calls=%fused_computation | custom fusion | bytes 1052672 | tf_op jit(solution)/shard_map/vmap()/gather | solution.py:55
  136.6 0.2 copy.20
  136.9 3.2 %gather_fusion.1 = bf16[512,256]{1,0:T(8,128)(2,1)S(1)} fusion(bf16[2,256,512]{1,2,0:T(8,128)(2,1)S(1)} %copy.20, s32[512]{0:T(512)S(1)} %bitcast.46), kind=kCustom, calls=%fused_computation.1 | custom fusion | bytes 528384 | tf_op jit(solution)/shard_map/vmap()/gather | solution.py:55
  140.0 0.1 fusion.13
  140.2 0.2 copy.21
  140.4 2.5 %select_reduce_fusion.1 = bf16[16,256,256]{2,1,0:T(8,128)(2,1)} fusion(f32[2,256,256]{2,1,0:T(8,128)S(1)} %copy.21, pred[16,2]{1,0:T(8,128)(4,1)S(1)} %iota_compare_fusion), kind=kLoop, calls=%fused_computation.3 | loop fusion | flops 3145728 | bytes 2621472 | tf_op jit(solution)/shard_map/reduce_sum | solution.py:62
  142.8 0.0 reduce-scatter.2.cloned.1.call-update
  142.9 35.2 %reduce-scatter.2.cloned.1.call-done = bf16[2,256,256]{2,1,0:T(8,128)(2,1)} async-done(((bf16[16,256,256]{2,1,0:T(8,128)(2,1)}), bf16[2,256,256]{2,1,0:T(8,128)(2,1)}) %reduce-scatter.2.cloned.1.call-update) | async-done | bytes 262160 | tf_op jit(solution)/shard_map/reduce_scatter | solution.py:66
  (10 shorter events, 0.0 us)
Async XLA Ops:
  6.5 1.2 copy-start
  6.5 171.6 %reduce-scatter.2.cloned.1.call-start = ((), (), s32[]{:S(2)}) async-start(), calls=%async_computation.1 | async-start | bytes 2359296 | tf_op jit(solution)/shard_map/reduce_scatter | solution.py:66
  19.0 9.9 %copy-start.3 = (s32[2,4]{1,0:T(2,128)S(1)}, s32[2,4]{1,0:T(2,128)}, u32[]{:S(2)}) copy-start(s32[2,4]{1,0:T(2,128)} %param.16) | copy-start | bytes 100
  44.7 22.5 %copy-start.1 = (bf16[2,512,512]{2,1,0:T(8,128)(2,1)S(1)}, bf16[2,512,512]{2,1,0:T(8,128)(2,1)}, u32[]{:S(2)}) copy-start(bf16[2,512,512]{2,1,0:T(8,128)(2,1)} %param.10) | copy-start | bytes 3145732
  44.7 23.1 %copy-start.2 = (s32[2,256]{1,0:T(2,128)S(1)}, s32[2,256]{1,0:T(2,128)}, u32[]{:S(2)}) copy-start(s32[2,256]{1,0:T(2,128)} %param.17) | copy-start | bytes 6148
  44.7 23.1 %copy-start.5 = (s32[2]{0:T(128)S(1)}, s32[2]{0:T(128)}, u32[]{:S(2)}) copy-start(s32[2]{0:T(128)} %param.18) | copy-start | bytes 28
  44.7 23.2 %copy-start.4 = (s32[2]{0:T(128)S(1)}, s32[2]{0:T(128)}, u32[]{:S(2)}) copy-start(s32[2]{0:T(128)} %param.19) | copy-start | bytes 28
  49.1 30.9 %collective-permute-start = (bf16[2,512,512]{1,2,0:T(8,128)(2,1)}, bf16[2,512,512]{1,2,0:T(8,128)(2,1)}, u32[]{:S(2)}, u32[]{:S(2)}) collective-permute-start(bf16[2,512,512]{1,2,0:T(8,128)(2,1)} %get-tuple-element.5), channel_id=1, source_target_pairs={{0,1},{1,2},{2,3},{3,4},{4,5},{5,6},{6,7},{7,8},{8,9},{9,10},{10,1... | collective-permute-start | bytes 3145736 | tf_op jit(solution)/shard_map/ppermute | solution.py:12
  52.6 29.4 %collective-permute-start.1 = (bf16[2,512,512]{1,2,0:T(8,128)(2,1)}, bf16[2,512,512]{1,2,0:T(8,128)(2,1)}, u32[]{:S(2)}, u32[]{:S(2)}) collective-permute-start(bf16[2,512,512]{1,2,0:T(8,128)(2,1)} %get-tuple-element.7), channel_id=1, source_target_pairs={{1,0},{2,1},{3,2},{4,3},{5,4},{6,5},{7,6},{8,7},{9,8},{10,9},{11,1... | collective-permute-start | bytes 3145736 | tf_op jit(solution)/shard_map/ppermute | solution.py:12
  58.7 45.8 %collective-permute-start.2 = (bf16[2,512,512]{1,2,0:T(8,128)(2,1)}, bf16[2,512,512]{1,2,0:T(8,128)(2,1)}, u32[]{:S(2)}, u32[]{:S(2)}) collective-permute-start(bf16[2,512,512]{1,2,0:T(8,128)(2,1)} %get-tuple-element.6), channel_id=1, source_target_pairs={{0,2},{1,3},{2,4},{3,5},{4,6},{5,7},{6,8},{7,9},{8,10},{9,11},{10,... | collective-permute-start | bytes 3145736 | tf_op jit(solution)/shard_map/ppermute | solution.py:12
  60.6 65.1 %collective-permute-start.3 = (bf16[2,512,512]{1,2,0:T(8,128)(2,1)}, bf16[2,512,512]{1,2,0:T(8,128)(2,1)}, u32[]{:S(2)}, u32[]{:S(2)}) collective-permute-start(bf16[2,512,512]{1,2,0:T(8,128)(2,1)} %get-tuple-element.8), channel_id=1, source_target_pairs={{2,0},{3,1},{4,2},{5,3},{6,4},{7,5},{8,6},{9,7},{10,8},{11,9},{12,... | collective-permute-start | bytes 3145736 | tf_op jit(solution)/shard_map/ppermute | solution.py:12
Sparse Core Ops, SparseCore 0:
  143.0 35.0 reduce-scatter.1
where the time goes:
time: 189 us; the launch traced here: 185 us
  waiting for transfers between devices  93.1 us (49%)
  local copies, waits for them, and re-layouts  32.4 us (17%)
  starting transfers between devices  18.1 us (10%)
  matrix products  16.7 us (9%)
  between operations  13.5 us (7%)
  other arithmetic  11.1 us (6%)
    ppermute x4, waiting for transfers between devices, from_behind(): return lax.ppermute(value, axis, pairs)  57.9 us
    reduce_scatter x1, waiting for transfers between devices, local(): lax.psum_scatter(placed.astype(jnp.bfloat16), 'region', scatter_dimension...  35.2 us
    ppermute x4, starting transfers between devices, from_behind(): return lax.ppermute(value, axis, pairs)  18.1 us
    dot_general x1, matrix products, local(): jnp.einsum('lksa,lkat->lkst', adjacent_discard_to_kept, reduced, preferre...  11.2 us
    dot_general x1, local copies, waits for them, and re-layouts, local(): jnp.einsum('lksa,lkat->lkst', adjacent_discard_to_kept, reduced, preferre...  9.92 us
    reduce_sum x1, other arithmetic, local(): jnp.sum(jnp.where(hits[:, :, :, None, None], near_update[:, :, None], jnp...  8.38 us
    gather x3, local copies, waits for them, and re-layouts, local(): dense_submatrix[element_slot][:, element_slot]  7.29 us
    reduce_sum x1, local copies, waits for them, and re-layouts, local(): jnp.sum(jnp.where(hits[:, :, :, None, None], near_update[:, :, None], jnp...  7.27 us
  transfers between devices with their start and end apart: 5, of which 5 were waited for; matrix products, arithmetic and copies ran while one was open for 0% of the time, Pallas kernels for 0%

commit v1 on v0

v1 whole, which is shorter than its diff:
```python
import functools

import jax
import jax.numpy as jnp
from jax import lax
from jax.experimental import pallas as pl
from jax.experimental.pallas import tpu as pltpu
from jax.sharding import PartitionSpec as P

offsets_list = (1, -1, 2, -2)
CODE_ROWS = 16
VMEM = pl.BlockSpec(memory_space=pltpu.VMEM)
HBM = pl.BlockSpec(memory_space=pltpu.HBM)
SMEM = pl.BlockSpec(memory_space=pltpu.SMEM)
LIMIT = 16 * 1024 * 1024
NEAR_LIMIT = 16 * 1024 * 1024


def shift(value, axis, by):
    length = lax.axis_size(axis)
    return lax.ppermute(value, axis, [(i, (i + by) % length) for i in range(length)])


def dot(a, b):
    return jnp.dot(a, b, preferred_element_type=jnp.float32)


def pickers(slots, span):
    count = slots.shape[1]
    column = lax.broadcasted_iota(jnp.int32, (span, count), 0) == slots
    tall = jnp.broadcast_to(slots, (128, count)).T
    lane = lax.broadcasted_iota(jnp.int32, (count, 128), 1)
    row = [tall == lane + at for at in range(0, span, 128)]
    one, zero = jnp.float32(1.0), jnp.float32(0.0)
    columns = jnp.where(column, one, zero).astype(jnp.bfloat16)
    rows = jnp.concatenate([jnp.where(r, one, zero).astype(jnp.bfloat16) for r in row], axis=1)
    return columns, rows


def self_kernel(slots_ref, tile_ref, inverse_ref, by_kept_ref, by_discard_ref, base_ref):
    place = pl.program_id(0)
    slots = jnp.where(place == 0, slots_ref[0:1, :], slots_ref[1:2, :])
    columns, rows = pickers(slots, tile_ref.shape[1])
    picked = dot(by_kept_ref[0], columns).astype(jnp.bfloat16)
    solved = dot(inverse_ref[0], picked).astype(jnp.bfloat16)
    left = dot(rows, by_discard_ref[0]).astype(jnp.bfloat16)
    tile = dot(rows, dot(tile_ref[0], columns).astype(jnp.bfloat16))
    base_ref[0] = tile - dot(left, solved)


def near_kernel(
    first,
    table_ref,
    one_ref,
    two_ref,
    inverse_ref,
    right_ref,
    left_ref,
    out_one,
    out_two,
    inverse,
    right,
    left,
    site_ref,
    sems,
):
    pairs = [(which, place) for which in range(2) for place in range(2)]
    copies = {}

    def copy(name, source, out):
        copies[name] = pltpu.make_async_copy(source, out, sems.at[len(copies)])
        copies[name].start()

    copy("site", table_ref, site_ref)
    for at, (which, place) in enumerate(pairs):
        copy(("right", at), right_ref.at[place, first + which], right.at[at])
    for place in range(2):
        copy(("inverse", place), inverse_ref.at[place], inverse.at[place])
    for at, (which, place) in enumerate(pairs):
        copy(("left", at), left_ref.at[place, first + which], left.at[at])

    copies["site"].wait()
    position = lax.axis_index("box")
    targets, columns, rows = [], [], []
    for which, place in pairs:
        there = position + offsets_list[first + which]
        inside = (there >= 0) & (there < lax.axis_size("box"))
        target = jnp.where(inside, site_ref[place, first + which], 2)
        slots_ref = (one_ref, two_ref)[which]
        column, row = pickers(
            jnp.where(target == 0, slots_ref[0:1], slots_ref[1:2]), left_ref.shape[2]
        )
        targets.append(target)
        columns.append(column)
        rows.append(row)

    for at in range(4):
        copies["right", at].wait()
    picked = [dot(right[at], columns[at]).astype(jnp.bfloat16) for at in range(4)]
    for place in range(2):
        copies["inverse", place].wait()
    reduced = [dot(inverse[place], picked[at]).astype(jnp.bfloat16) for at, (_, place) in enumerate(pairs)]
    for at in range(4):
        copies["left", at].wait()
    coupled = [dot(rows[at], left[at]).astype(jnp.bfloat16) for at in range(4)]
    near = [dot(coupled[at], reduced[at]) for at in range(4)]
    for which, out in enumerate((out_one, out_two)):
        for t in range(2):
            terms = [jnp.where(targets[2 * which + p] == t, near[2 * which + p], 0.0) for p in range(2)]
            out[t] = (terms[0] + terms[1]).astype(out.dtype)


def add_kernel(near_one, near_two, far_one, far_two, out_one, out_two):
    for near, far, out in ((near_one, far_one, out_one), (near_two, far_two, out_two)):
        out[...] = (near[...] + far[...].astype(jnp.float32)).astype(jnp.bfloat16)


def child_kernel(length_ref, code_ref, base_ref, a_ref, b_ref, out_ref):
    span = base_ref.shape[1]
    for place in range(base_ref.shape[0]):
        value = base_ref[place]
        for ref in (a_ref, b_ref):
            value = value - ref[place].astype(jnp.float32)
        length = length_ref[place]
        row = lax.broadcasted_iota(jnp.int32, (span, span), 0)
        column = lax.broadcasted_iota(jnp.int32, (span, span), 1)
        valid = (row < length) & (column < length)
        out_ref[place, 0:span] = jnp.where(valid, value, 0.0).astype(jnp.bfloat16)
        code = code_ref[place].astype(jnp.float32)
        out_ref[place, span:] = jnp.full((CODE_ROWS, span), code, jnp.float32).astype(jnp.bfloat16)


def choose_kernel(a_ref, b_ref, c_ref, d_ref, mine_ref, other_ref):
    span = mine_ref.shape[1]
    region = lax.axis_index("region")
    partner = region + 1 - 2 * lax.rem(region, 2)
    for out_ref, owner in ((mine_ref, region), (other_ref, partner)):
        for slot in range(2):
            wanted = (owner * 2 + slot).astype(jnp.float32)
            value = None
            for ref in (a_ref, b_ref, c_ref, d_ref):
                for place in range(2):
                    code = ref[place, span : span + 1, :].astype(jnp.float32)
                    hit = jnp.where(code == wanted, 1.0, 0.0).astype(jnp.bfloat16)
                    term = ref[place, 0:span] * hit
                    value = term if value is None else value + term
            out_ref[slot] = value


def join_kernel(a_ref, b_ref, out_ref):
    out_ref[...] = a_ref[...] + b_ref[...]


def local(
    kept_diagonal_tile,
    discard_reciprocal,
    discard_by_kept,
    kept_by_discard,
    adjacent_discard_to_kept,
    adjacent_kept_to_discard,
    adjacent_site_table,
    retained_slots,
    kept_list_length,
    ancestor_site_map,
):
    places, tile_span = retained_slots.shape
    wide, tall = kept_diagonal_tile.shape[1], discard_reciprocal.shape[1]
    params = pltpu.CompilerParams(vmem_limit_bytes=LIMIT)
    small = jax.ShapeDtypeStruct((places, tile_span, tile_span), jnp.bfloat16)

    def block(rows, columns):
        return pl.BlockSpec((1, rows, columns), lambda l: (l, 0, 0))

    def self_update():
        return pl.pallas_call(
            self_kernel,
            grid=(places,),
            in_specs=[VMEM, block(wide, wide), block(tall, tall), block(tall, wide), block(wide, tall)],
            out_specs=block(tile_span, tile_span),
            out_shape=jax.ShapeDtypeStruct((places, tile_span, tile_span), jnp.float32),
            compiler_params=params,
            name="self_update",
        )(retained_slots, kept_diagonal_tile, discard_reciprocal, discard_by_kept, kept_by_discard)

    def slots_of(first):
        return [shift(retained_slots, "box", -offsets_list[first + i]) for i in range(2)]

    def near(first, slots, dtype):
        shape = jax.ShapeDtypeStruct((places, tile_span, tile_span), dtype)
        return pl.pallas_call(
            functools.partial(near_kernel, first),
            in_specs=[HBM, VMEM, VMEM, HBM, HBM, HBM],
            out_specs=[VMEM, VMEM],
            out_shape=[shape, shape],
            scratch_shapes=[
                pltpu.VMEM((2, tall, tall), jnp.bfloat16),
                pltpu.VMEM((4, tall, wide), jnp.bfloat16),
                pltpu.VMEM((4, wide, tall), jnp.bfloat16),
                pltpu.SMEM(adjacent_site_table.shape, jnp.int32),
                pltpu.SemaphoreType.DMA((11,)),
            ],
            compiler_params=pltpu.CompilerParams(vmem_limit_bytes=NEAR_LIMIT),
            name="near_update",
        )(
            pltpu.with_memory_space_constraint(adjacent_site_table, pltpu.HBM),
            *slots,
            *[pltpu.with_memory_space_constraint(v, pltpu.HBM) for v in (discard_reciprocal, adjacent_kept_to_discard, adjacent_discard_to_kept)],
        )

    far_slots, near_slots = lax.optimization_barrier((slots_of(2), slots_of(0)))
    far_one, far_two = near(2, far_slots, jnp.bfloat16)
    passed = [shift(far_one, "box", 1), shift(far_two, "box", -1)]
    near_one, near_two = near(0, near_slots, jnp.float32)
    sent = pl.pallas_call(
        add_kernel,
        in_specs=[VMEM] * 4,
        out_specs=[VMEM] * 2,
        out_shape=[small, small],
        compiler_params=params,
        name="add",
    )(near_one, near_two, *passed)
    arrived = [shift(sent[0], "box", 1), shift(sent[1], "box", -1)]
    base = self_update()

    child = pl.pallas_call(
        child_kernel,
        in_specs=[SMEM, SMEM] + [VMEM] * 3,
        out_specs=VMEM,
        out_shape=jax.ShapeDtypeStruct((places, tile_span + CODE_ROWS, tile_span), jnp.bfloat16),
        compiler_params=params,
        name="child",
    )(kept_list_length, ancestor_site_map, base, *arrived)

    gathered = [child] + [shift(child, "region", by) for by in (2, -2, 4)]
    mine, other = pl.pallas_call(
        choose_kernel,
        in_specs=[VMEM] * 4,
        out_specs=[VMEM, VMEM],
        out_shape=[small, small],
        compiler_params=params,
        name="choose",
    )(*gathered)
    partners = [(i, i ^ 1) for i in range(lax.axis_size("region"))]
    received = lax.ppermute(other, "region", partners)
    return pl.pallas_call(
        join_kernel,
        in_specs=[VMEM] * 2,
        out_specs=VMEM,
        out_shape=small,
        compiler_params=params,
        name="join",
    )(mine, received)


def solution(mesh):
    in_specs = (
        P(("region", "box"), None, None),
        P(("region", "box"), None, None),
        P(("region", "box"), None, None),
        P(("region", "box"), None, None),
        P(("region", "box"), None, None, None),
        P(("region", "box"), None, None, None),
        P(("region", "box"), None),
        P(("region", "box"), None),
        P(("region", "box")),
        P(("region", "box")),
    )
    out_specs = P(("region", "box"), None, None)
    return jax.shard_map(local, mesh=mesh, in_specs=in_specs, out_specs=out_specs, check_vma=False)
```

time: 189 us -> 62.1 us (0.33)
  the two profiles are of different devices: /device:TPU:25 before, /device:TPU:1 now
where the time goes in v1:
time: 62.1 us; the launch traced here: 62 us
  starting transfers between devices  35.5 us (57%)
  waiting for transfers between devices  14.1 us (23%)
  Pallas kernels  12.2 us (20%)
    ppermute x11, starting transfers between devices, shift(): lax.ppermute(value, axis, [(i, (i + by) % length) for i in range(length)])  29.8 us
    ppermute x11, waiting for transfers between devices, shift(): lax.ppermute(value, axis, [(i, (i + by) % length) for i in range(length)])  13 us
    pallas_call x2, Pallas kernels, near(): pl.pallas_call(functools.partial(near_kernel, first), in_specs=[HBM, VMEM...  8.03 us
    ppermute x1, starting transfers between devices, local(): received = lax.ppermute(other, 'region', partners)  5.67 us
    pallas_call x1, Pallas kernels, self_update(): pl.pallas_call(self_kernel, grid=(places,), in_specs=[VMEM, block(wide, w...  2.36 us
  transfers between devices with their start and end apart: 12, of which 7 were waited for; matrix products, arithmetic and copies ran while one was open for 0% of the time, Pallas kernels for 10%

profile of v1, /device:TPU:1, one launch (start us, length us, event | category | flops | bytes accessed | tf_op | source)
XLA Modules:
  0.0 62.0 jit_solution(807318554684170694)
XLA Ops:
  0.0 9.3 %collective-permute-start = (s32[2,256]{1,0:T(2,128)}, s32[2,256]{1,0:T(2,128)S(1)}, u32[]{:S(2)}, u32[]{:S(2)}) collective-permute-start(s32[2,256]{1,0:T(2,128)} %slots_ref.1), channel_id=1, source_target_pairs={{0,30},{1,31},{2,0},{3,1},{4,2},{5,3},{6,4},{7,5},{8,6},{9,7},{10,... | collective-permute-start | bytes 6152 | tf_op jit(solution)/shard_map/ppermute | solution.py:21
  9.3 5.2 %collective-permute-start.2 = (s32[2,256]{1,0:T(2,128)}, s32[2,256]{1,0:T(2,128)S(1)}, u32[]{:S(2)}, u32[]{:S(2)}) collective-permute-start(s32[2,256]{1,0:T(2,128)} %slots_ref.1), channel_id=1, source_target_pairs={{0,31},{1,0},{2,1},{3,2},{4,3},{5,4},{6,5},{7,6},{8,7},{9,8},{10,9... | collective-permute-start | bytes 6152 | tf_op jit(solution)/shard_map/ppermute | solution.py:21
  14.5 1.6 %collective-permute-done.1.two_ref = s32[2,256]{1,0:T(2,128)S(1)} collective-permute-done((s32[2,256]{1,0:T(2,128)}, s32[2,256]{1,0:T(2,128)S(1)}, u32[]{:S(2)}, u32[]{:S(2)}) %collective-permute-start.1) | collective-permute-done | bytes 2080 | tf_op jit(solution)/shard_map/ppermute | solution.py:21
  16.2 0.0 collective-permute-done.2.one_ref
  16.2 4.3 %collective-permute-done.3.two_ref = s32[2,256]{1,0:T(2,128)S(1)} collective-permute-done((s32[2,256]{1,0:T(2,128)}, s32[2,256]{1,0:T(2,128)S(1)}, u32[]{:S(2)}, u32[]{:S(2)}) %collective-permute-start.3) | collective-permute-done | bytes 2080 | tf_op jit(solution)/shard_map/ppermute | solution.py:21
  20.5 4.0 %near_update.3 = (bf16[2,256,256]{2,1,0:T(8,128)(2,1)S(1)}, bf16[2,256,256]{2,1,0:T(8,128)(2,1)S(1)}) custom-call(s32[2,4]{1,0:T(2,128)} %table_ref.3, s32[2,256]{1,0:T(2,128)S(1)} %collective-permute-done.one_ref, s32[2,256]{1,0:T(2,128)S(1)} %collective-permute-done.1.two_ref, bf16[2,512,512]{2,1,0:T(8,128)(2,1)} %inverse_ref.5, ...), custom_call_target="tpu_custom_call" | custom-call | tf_op jit(solution)/shard_map/near_update/pallas_call | solution.py:190
  24.5 0.1 collective-permute-start.4
  24.6 0.0 copy-start
  24.6 0.0 copy-start.1
  24.6 0.0 copy-start.2
  24.7 0.0 copy-start.3
  24.7 0.0 copy-start.4
  24.7 4.8 %collective-permute-start.5 = (bf16[2,256,256]{2,1,0:T(8,128)(2,1)S(1)}, bf16[2,256,256]{2,1,0:T(8,128)(2,1)S(1)}, u32[]{:S(2)}, u32[]{:S(2)}) collective-permute-start(bf16[2,256,256]{2,1,0:T(8,128)(2,1)S(1)} %get-tuple-element.24), channel_id=1, source_target_pairs={{0,31},{1,0},{2,1},{3,2},{4,3},{5,4},{6,5},{7,6},{8,7},{9,8},{10,9... | collective-permute-start | bytes 786440 | tf_op jit(solution)/shard_map/ppermute | solution.py:21
  29.5 4.0 %near_update.2 = (f32[2,256,256]{2,1,0:T(8,128)S(1)}, f32[2,256,256]{2,1,0:T(8,128)S(1)}) custom-call(s32[2,4]{1,0:T(2,128)} %table_ref.3, s32[2,256]{1,0:T(2,128)S(1)} %collective-permute-done.2.one_ref, s32[2,256]{1,0:T(2,128)S(1)} %collective-permute-done.3.two_ref, bf16[2,512,512]{2,1,0:T(8,128)(2,1)} %inverse_ref.5, bf16[2,4,512,512]{3,2,1,0:T(8,128)(2,1)} %right_ref.3, ...), custom_call_target="tpu_custom_call" | custom-call | tf_op jit(solution)/shard_map/near_update/pallas_call | solution.py:190
  33.5 0.0 copy-start.5
  33.5 0.0 copy-start.6
  33.6 0.1 add.1
  33.7 0.1 collective-permute-start.6
  33.8 4.8 %collective-permute-start.7 = (bf16[2,256,256]{2,1,0:T(8,128)(2,1)S(1)}, bf16[2,256,256]{2,1,0:T(8,128)(2,1)S(1)}, u32[]{:S(2)}, u32[]{:S(2)}) collective-permute-start(bf16[2,256,256]{2,1,0:T(8,128)(2,1)S(1)} %get-tuple-element.26), channel_id=1, source_target_pairs={{0,31},{1,0},{2,1},{3,2},{4,3},{5,4},{6,5},{7,6},{8,7},{9,8},{10,9... | collective-permute-start | bytes 786440 | tf_op jit(solution)/shard_map/ppermute | solution.py:21
  38.6 2.4 %self_update.1.base_ref = f32[2,256,256]{2,1,0:T(8,128)S(1)} custom-call(s32[2,256]{1,0:T(2,128)S(1)} %copy-done.4, bf16[2,512,512]{2,1,0:T(8,128)(2,1)S(1)} %copy-done.1, bf16[2,512,512]{2,1,0:T(8,128)(2,1)S(1)} %copy-done, bf16[2,512,512]{2,1,0:T(8,128)(2,1)S(1)} %copy-done.2, bf16[2,512,512]{2,1,0:T(8,128)(2,1)S(1)} %copy-done.3), custom_call_target="tpu_custom_call" | custom-call | tf_op jit(solution)/shard_map/self_update/pallas_call | solution.py:175
  40.9 1.4 %collective-permute-done.6.a_ref = bf16[2,256,256]{2,1,0:T(8,128)(2,1)S(1)} collective-permute-done((bf16[2,256,256]{2,1,0:T(8,128)(2,1)S(1)}, bf16[2,256,256]{2,1,0:T(8,128)(2,1)S(1)}, u32[]{:S(2)}, u32[]{:S(2)}) %collective-permute-start.6) | collective-permute-done | bytes 262176 | tf_op jit(solution)/shard_map/ppermute | solution.py:21
  42.3 0.7 %child.1.a_ref = bf16[2,272,256]{2,1,0:T(8,128)(2,1)S(1)} custom-call(s32[2]{0:T(128)S(1)} %copy-done.5, s32[2]{0:T(128)S(1)} %copy-done.6, f32[2,256,256]{2,1,0:T(8,128)S(1)} %self_update.1.base_ref, bf16[2,256,256]{2,1,0:T(8,128)(2,1)S(1)} %collective-permute-done.6.a_ref, bf16[2,256,256]{2,1,0:T(8,128)(2,1)S(1)} %collective-permute-done.7.b_ref), custom_call_target="tpu_custom_call" | custom-call | tf_op jit(solution)/shard_map/child/pallas_call | solution.py:225
  43.0 2.8 %collective-permute-start.10 = (bf16[2,272,256]{2,1,0:T(8,128)(2,1)S(1)}, bf16[2,272,256]{2,1,0:T(8,128)(2,1)S(1)}, u32[]{:S(2)}, u32[]{:S(2)}) collective-permute-start(bf16[2,272,256]{2,1,0:T(8,128)(2,1)S(1)} %child.1.a_ref), channel_id=1, source_target_pairs={{0,128},{32,160},{64,192},{96,224},{128,0},{160,32},{192,64},{224,... | collective-permute-start | bytes 835592 | tf_op jit(solution)/shard_map/ppermute | solution.py:21
  45.8 0.3 collective-permute-start.8
  46.1 2.4 %collective-permute-start.9 = (bf16[2,272,256]{2,1,0:T(8,128)(2,1)S(1)}, bf16[2,272,256]{2,1,0:T(8,128)(2,1)S(1)}, u32[]{:S(2)}, u32[]{:S(2)}) collective-permute-start(bf16[2,272,256]{2,1,0:T(8,128)(2,1)S(1)} %child.1.a_ref), channel_id=1, source_target_pairs={{0,192},{32,224},{64,0},{96,32},{128,64},{160,96},{192,128},{224,1... | collective-permute-start | bytes 835592 | tf_op jit(solution)/shard_map/ppermute | solution.py:21
  48.5 1.5 %collective-permute-done.10.d_ref = bf16[2,272,256]{2,1,0:T(8,128)(2,1)S(1)} collective-permute-done((bf16[2,272,256]{2,1,0:T(8,128)(2,1)S(1)}, bf16[2,272,256]{2,1,0:T(8,128)(2,1)S(1)}, u32[]{:S(2)}, u32[]{:S(2)}) %collective-permute-start.10) | collective-permute-done | bytes 278560 | tf_op jit(solution)/shard_map/ppermute | solution.py:21
  50.0 4.0 %collective-permute-done.8.b_ref = bf16[2,272,256]{2,1,0:T(8,128)(2,1)S(1)} collective-permute-done((bf16[2,272,256]{2,1,0:T(8,128)(2,1)S(1)}, bf16[2,272,256]{2,1,0:T(8,128)(2,1)S(1)}, u32[]{:S(2)}, u32[]{:S(2)}) %collective-permute-start.8) | collective-permute-done | bytes 278560 | tf_op jit(solution)/shard_map/ppermute | solution.py:21
  54.0 0.1 collective-permute-done.9.c_ref
  54.1 0.3 choose.1
  54.4 5.7 %collective-permute-start.11 = (bf16[2,256,256]{2,1,0:T(8,128)(2,1)S(1)}, bf16[2,256,256]{2,1,0:T(8,128)(2,1)S(1)}, u32[]{:S(2)}, u32[]{:S(2)}) collective-permute-start(bf16[2,256,256]{2,1,0:T(8,128)(2,1)S(1)} %get-tuple-element.28), channel_id=1, source_target_pairs={{0,32},{32,0},{64,96},{96,64},{128,160},{160,128},{192,224},{224,1... | collective-permute-start | bytes 786440 | tf_op jit(solution)/shard_map/ppermute | solution.py:244
  60.1 1.2 %collective-permute-done.11.b_ref = bf16[2,256,256]{2,1,0:T(8,128)(2,1)S(1)} collective-permute-done((bf16[2,256,256]{2,1,0:T(8,128)(2,1)S(1)}, bf16[2,256,256]{2,1,0:T(8,128)(2,1)S(1)}, u32[]{:S(2)}, u32[]{:S(2)}) %collective-permute-start.11) | collective-permute-done | bytes 262176 | tf_op jit(solution)/shard_map/ppermute | solution.py:244
  61.3 0.7 %join.1 = bf16[2,256,256]{2,1,0:T(8,128)(2,1)} custom-call(bf16[2,256,256]{2,1,0:T(8,128)(2,1)S(1)} %get-tuple-element.27.a_ref, bf16[2,256,256]{2,1,0:T(8,128)(2,1)S(1)} %collective-permute-done.11.b_ref), custom_call_target="tpu_custom_call" | custom-call | tf_op jit(solution)/shard_map/join/pallas_call | solution.py:245
  (13 shorter events, 0.0 us)
Async XLA Ops:
  0.0 14.5 %collective-permute-start = (s32[2,256]{1,0:T(2,128)}, s32[2,256]{1,0:T(2,128)S(1)}, u32[]{:S(2)}, u32[]{:S(2)}) collective-permute-start(s32[2,256]{1,0:T(2,128)} %slots_ref.1), channel_id=1, source_target_pairs={{0,30},{1,31},{2,0},{3,1},{4,2},{5,3},{6,4},{7,5},{8,6},{9,7},{10,... | collective-permute-start | bytes 6152 | tf_op jit(solution)/shard_map/ppermute | solution.py:21
  9.3 6.9 %collective-permute-start.1 = (s32[2,256]{1,0:T(2,128)}, s32[2,256]{1,0:T(2,128)S(1)}, u32[]{:S(2)}, u32[]{:S(2)}) collective-permute-start(s32[2,256]{1,0:T(2,128)} %slots_ref.1), channel_id=1, source_target_pairs={{0,2},{1,3},{2,4},{3,5},{4,6},{5,7},{6,8},{7,9},{8,10},{9,11},{10,... | collective-permute-start | bytes 6152 | tf_op jit(solution)/shard_map/ppermute | solution.py:21
  9.3 6.9 %collective-permute-start.2 = (s32[2,256]{1,0:T(2,128)}, s32[2,256]{1,0:T(2,128)S(1)}, u32[]{:S(2)}, u32[]{:S(2)}) collective-permute-start(s32[2,256]{1,0:T(2,128)} %slots_ref.1), channel_id=1, source_target_pairs={{0,31},{1,0},{2,1},{3,2},{4,3},{5,4},{6,5},{7,6},{8,7},{9,8},{10,9... | collective-permute-start | bytes 6152 | tf_op jit(solution)/shard_map/ppermute | solution.py:21
  14.5 6.0 %collective-permute-start.3 = (s32[2,256]{1,0:T(2,128)}, s32[2,256]{1,0:T(2,128)S(1)}, u32[]{:S(2)}, u32[]{:S(2)}) collective-permute-start(s32[2,256]{1,0:T(2,128)} %slots_ref.1), channel_id=1, source_target_pairs={{0,1},{1,2},{2,3},{3,4},{4,5},{5,6},{6,7},{7,8},{8,9},{9,10},{10,1... | collective-permute-start | bytes 6152 | tf_op jit(solution)/shard_map/ppermute | solution.py:21
  24.5 9.0 %collective-permute-start.4 = (bf16[2,256,256]{2,1,0:T(8,128)(2,1)S(1)}, bf16[2,256,256]{2,1,0:T(8,128)(2,1)S(1)}, u32[]{:S(2)}, u32[]{:S(2)}) collective-permute-start(bf16[2,256,256]{2,1,0:T(8,128)(2,1)S(1)} %get-tuple-element.23), channel_id=1, source_target_pairs={{0,1},{1,2},{2,3},{3,4},{4,5},{5,6},{6,7},{7,8},{8,9},{9,10},{10,1... | collective-permute-start | bytes 786440 | tf_op jit(solution)/shard_map/ppermute | solution.py:21
  24.6 13.9 %copy-start = (bf16[2,512,512]{2,1,0:T(8,128)(2,1)S(1)}, bf16[2,512,512]{2,1,0:T(8,128)(2,1)}, u32[]{:S(2)}) copy-start(bf16[2,512,512]{2,1,0:T(8,128)(2,1)} %inverse_ref.5) | copy-start | bytes 3145732
  24.6 13.9 %copy-start.1 = (bf16[2,512,512]{2,1,0:T(8,128)(2,1)S(1)}, bf16[2,512,512]{2,1,0:T(8,128)(2,1)}, u32[]{:S(2)}) copy-start(bf16[2,512,512]{2,1,0:T(8,128)(2,1)} %tile_ref.1) | copy-start | bytes 3145732
  24.6 13.9 %copy-start.2 = (bf16[2,512,512]{2,1,0:T(8,128)(2,1)S(1)}, bf16[2,512,512]{2,1,0:T(8,128)(2,1)}, u32[]{:S(2)}) copy-start(bf16[2,512,512]{2,1,0:T(8,128)(2,1)} %by_kept_ref.1) | copy-start | bytes 3145732
  24.7 13.9 %copy-start.3 = (bf16[2,512,512]{2,1,0:T(8,128)(2,1)S(1)}, bf16[2,512,512]{2,1,0:T(8,128)(2,1)}, u32[]{:S(2)}) copy-start(bf16[2,512,512]{2,1,0:T(8,128)(2,1)} %by_discard_ref.1) | copy-start | bytes 3145732
  24.7 13.9 %copy-start.4 = (s32[2,256]{1,0:T(2,128)S(1)}, s32[2,256]{1,0:T(2,128)}, u32[]{:S(2)}) copy-start(s32[2,256]{1,0:T(2,128)} %slots_ref.1) | copy-start | bytes 6148
  24.7 8.9 %collective-permute-start.5 = (bf16[2,256,256]{2,1,0:T(8,128)(2,1)S(1)}, bf16[2,256,256]{2,1,0:T(8,128)(2,1)S(1)}, u32[]{:S(2)}, u32[]{:S(2)}) collective-permute-start(bf16[2,256,256]{2,1,0:T(8,128)(2,1)S(1)} %get-tuple-element.24), channel_id=1, source_target_pairs={{0,31},{1,0},{2,1},{3,2},{4,3},{5,4},{6,5},{7,6},{8,7},{9,8},{10,9... | collective-permute-start | bytes 786440 | tf_op jit(solution)/shard_map/ppermute | solution.py:21
  33.5 8.8 %copy-start.5 = (s32[2]{0:T(128)S(1)}, s32[2]{0:T(128)}, u32[]{:S(2)}) copy-start(s32[2]{0:T(128)} %length_ref.1) | copy-start | bytes 28
  33.5 8.8 %copy-start.6 = (s32[2]{0:T(128)S(1)}, s32[2]{0:T(128)}, u32[]{:S(2)}) copy-start(s32[2]{0:T(128)} %code_ref.1) | copy-start | bytes 28
  33.7 8.6 %collective-permute-start.6 = (bf16[2,256,256]{2,1,0:T(8,128)(2,1)S(1)}, bf16[2,256,256]{2,1,0:T(8,128)(2,1)S(1)}, u32[]{:S(2)}, u32[]{:S(2)}) collective-permute-start(bf16[2,256,256]{2,1,0:T(8,128)(2,1)S(1)} %get-tuple-element.25), channel_id=1, source_target_pairs={{0,1},{1,2},{2,3},{3,4},{4,5},{5,6},{6,7},{7,8},{8,9},{9,10},{10,1... | collective-permute-start | bytes 786440 | tf_op jit(solution)/shard_map/ppermute | solution.py:21
  33.8 8.5 %collective-permute-start.7 = (bf16[2,256,256]{2,1,0:T(8,128)(2,1)S(1)}, bf16[2,256,256]{2,1,0:T(8,128)(2,1)S(1)}, u32[]{:S(2)}, u32[]{:S(2)}) collective-permute-start(bf16[2,256,256]{2,1,0:T(8,128)(2,1)S(1)} %get-tuple-element.26), channel_id=1, source_target_pairs={{0,31},{1,0},{2,1},{3,2},{4,3},{5,4},{6,5},{7,6},{8,7},{9,8},{10,9... | collective-permute-start | bytes 786440 | tf_op jit(solution)/shard_map/ppermute | solution.py:21
  43.0 7.0 %collective-permute-start.10 = (bf16[2,272,256]{2,1,0:T(8,128)(2,1)S(1)}, bf16[2,272,256]{2,1,0:T(8,128)(2,1)S(1)}, u32[]{:S(2)}, u32[]{:S(2)}) collective-permute-start(bf16[2,272,256]{2,1,0:T(8,128)(2,1)S(1)} %child.1.a_ref), channel_id=1, source_target_pairs={{0,128},{32,160},{64,192},{96,224},{128,0},{160,32},{192,64},{224,... | collective-permute-start | bytes 835592 | tf_op jit(solution)/shard_map/ppermute | solution.py:21
  45.8 8.2 %collective-permute-start.8 = (bf16[2,272,256]{2,1,0:T(8,128)(2,1)S(1)}, bf16[2,272,256]{2,1,0:T(8,128)(2,1)S(1)}, u32[]{:S(2)}, u32[]{:S(2)}) collective-permute-start(bf16[2,272,256]{2,1,0:T(8,128)(2,1)S(1)} %child.1.a_ref), channel_id=1, source_target_pairs={{0,64},{32,96},{64,128},{96,160},{128,192},{160,224},{192,0},{224,... | collective-permute-start | bytes 835592 | tf_op jit(solution)/shard_map/ppermute | solution.py:21
  46.1 8.0 %collective-permute-start.9 = (bf16[2,272,256]{2,1,0:T(8,128)(2,1)S(1)}, bf16[2,272,256]{2,1,0:T(8,128)(2,1)S(1)}, u32[]{:S(2)}, u32[]{:S(2)}) collective-permute-start(bf16[2,272,256]{2,1,0:T(8,128)(2,1)S(1)} %child.1.a_ref), channel_id=1, source_target_pairs={{0,192},{32,224},{64,0},{96,32},{128,64},{160,96},{192,128},{224,1... | collective-permute-start | bytes 835592 | tf_op jit(solution)/shard_map/ppermute | solution.py:21
  54.4 6.8 %collective-permute-start.11 = (bf16[2,256,256]{2,1,0:T(8,128)(2,1)S(1)}, bf16[2,256,256]{2,1,0:T(8,128)(2,1)S(1)}, u32[]{:S(2)}, u32[]{:S(2)}) collective-permute-start(bf16[2,256,256]{2,1,0:T(8,128)(2,1)S(1)} %get-tuple-element.28), channel_id=1, source_target_pairs={{0,32},{32,0},{64,96},{96,64},{128,160},{160,128},{192,224},{224,1... | collective-permute-start | bytes 786440 | tf_op jit(solution)/shard_map/ppermute | solution.py:244

commit v2 on v1

v2 whole, which is shorter than its diff:
```python
import functools

import jax
import jax.numpy as jnp
from jax import lax
from jax.experimental import pallas as pl
from jax.experimental.pallas import tpu as pltpu
from jax.sharding import PartitionSpec as P

offsets_list = (1, -1, 2, -2)
CODE_ROWS = 16
VMEM = pl.BlockSpec(memory_space=pltpu.VMEM)
HBM = pl.BlockSpec(memory_space=pltpu.HBM)
SMEM = pl.BlockSpec(memory_space=pltpu.SMEM)
LIMIT = 16 * 1024 * 1024
NEAR_LIMIT = 16 * 1024 * 1024


def shift(value, axis, by):
    length = lax.axis_size(axis)
    return lax.ppermute(value, axis, [(i, (i + by) % length) for i in range(length)])


def turn(value, by):
    regions, length = lax.axis_size("region"), lax.axis_size("box")
    pairs = []
    for r in range(regions):
        for j in range(length):
            there = j + (by if r % 2 == 0 else -by)
            goal = (r, there) if 0 <= there < length else (r + 1 - 2 * (r % 2), j)
            pairs.append((r * length + j, goal[0] * length + goal[1]))
    return lax.ppermute(value, ("region", "box"), pairs)


def dot(a, b):
    return jnp.dot(a, b, preferred_element_type=jnp.float32)


def pickers(slots, span):
    count = slots.shape[1]
    column = lax.broadcasted_iota(jnp.int32, (span, count), 0) == slots
    tall = jnp.broadcast_to(slots, (128, count)).T
    lane = lax.broadcasted_iota(jnp.int32, (count, 128), 1)
    row = [tall == lane + at for at in range(0, span, 128)]
    one, zero = jnp.float32(1.0), jnp.float32(0.0)
    columns = jnp.where(column, one, zero).astype(jnp.bfloat16)
    rows = jnp.concatenate([jnp.where(r, one, zero).astype(jnp.bfloat16) for r in row], axis=1)
    return columns, rows


def self_kernel(slots_ref, tile_ref, inverse_ref, by_kept_ref, by_discard_ref, base_ref):
    place = pl.program_id(0)
    slots = jnp.where(place == 0, slots_ref[0:1, :], slots_ref[1:2, :])
    columns, rows = pickers(slots, tile_ref.shape[1])
    picked = dot(by_kept_ref[0], columns).astype(jnp.bfloat16)
    solved = dot(inverse_ref[0], picked).astype(jnp.bfloat16)
    left = dot(rows, by_discard_ref[0]).astype(jnp.bfloat16)
    tile = dot(rows, dot(tile_ref[0], columns).astype(jnp.bfloat16))
    base_ref[0] = tile - dot(left, solved)


def directions():
    core = lax.rem(lax.axis_index("region"), 2)
    return core, 1 - core


def load_kernel(first, *refs):
    count = (len(refs) - 1) // 2
    sources, outs, sems = refs[:count], refs[count : 2 * count], refs[2 * count]
    copies = []

    def copy(source, out):
        copies.append(pltpu.make_async_copy(source, out, sems.at[len(copies)]))

    along = directions()
    for source, out in zip(sources, outs):
        if len(source.shape) == 4:
            for which in range(2):
                for place in range(2):
                    copy(source.at[place, first + along[which]], out.at[2 * which + place])
        else:
            copy(source, out)
    for each in copies:
        each.start()
    for each in copies:
        each.wait()


def near_kernel(first, span, slots_of, site_ref, inverse, right, left):
    along = directions()
    core = along[0]
    position = lax.axis_index("box")
    pairs = [(which, place) for which in range(2) for place in range(2)]
    targets, columns, rows = [], [], []
    for which, place in pairs:
        there = position + offsets_list[first] * (1 - 2 * along[which])
        inside = (there >= 0) & (there < lax.axis_size("box"))
        one, two = (site_ref[place : place + 1, first + i : first + i + 1] for i in (which, 1 - which))
        target = jnp.where(inside, jnp.where(core == 0, one, two), 2)
        slots = slots_of(which)
        column, row = pickers(jnp.where(target == 0, slots[0:1], slots[1:2]), span)
        targets.append(target)
        columns.append(column)
        rows.append(row)
    picked = [dot(right[at], columns[at]).astype(jnp.bfloat16) for at in range(4)]
    reduced = [dot(inverse[place], picked[at]).astype(jnp.bfloat16) for at, (_, place) in enumerate(pairs)]
    coupled = [dot(rows[at], left[at]).astype(jnp.bfloat16) for at in range(4)]
    near = [dot(coupled[at], reduced[at]) for at in range(4)]
    return [
        [sum(jnp.where(targets[2 * which + p] == t, near[2 * which + p], 0.0) for p in range(2)) for t in range(2)]
        for which in range(2)
    ]


def far_kernel(one_ref, two_ref, own_ref, site_ref, inverse, right, left, out_one, out_two):
    span = own_ref.shape[1]
    from_there = (two_ref, one_ref)
    updates = near_kernel(2, left.shape[1], lambda w: from_there[w][...], site_ref, inverse, right, left)
    own = own_ref[...]
    row = lax.broadcasted_iota(jnp.int32, (CODE_ROWS, span), 0)
    halves = (own >> 1, own & 1)
    code = jnp.zeros((CODE_ROWS, span), jnp.int32)
    for at in range(4):
        code = jnp.where(row == at, halves[at // 2][at % 2 : at % 2 + 1], code)
    code = code.astype(jnp.float32).astype(jnp.bfloat16)
    for out, update in zip((out_one, out_two), updates):
        for t in range(2):
            out[t * span : (t + 1) * span] = update[t].astype(jnp.bfloat16)
        out[2 * span :] = code


def step_kernel(one_ref, two_ref, site_ref, inverse, right, left, out_one, out_two):
    span = out_one.shape[1]
    passed = (one_ref, two_ref)

    def slots_of(which):
        code = passed[1 - which][2 * span :].astype(jnp.float32).astype(jnp.int32)
        return code[0:2] * 2 + code[2:4]

    updates = near_kernel(0, left.shape[1], slots_of, site_ref, inverse, right, left)
    for which, out in enumerate((out_one, out_two)):
        for t in range(2):
            far = passed[which][t * span : (t + 1) * span].astype(jnp.float32)
            out[t] = (updates[which][t] + far).astype(jnp.bfloat16)


def child_kernel(length_ref, code_ref, base_ref, a_ref, b_ref, out_ref):
    span = base_ref.shape[1]
    for place in range(base_ref.shape[0]):
        value = base_ref[place]
        for ref in (a_ref, b_ref):
            value = value - ref[place].astype(jnp.float32)
        length = length_ref[place]
        row = lax.broadcasted_iota(jnp.int32, (span, span), 0)
        column = lax.broadcasted_iota(jnp.int32, (span, span), 1)
        valid = (row < length) & (column < length)
        out_ref[place * span : (place + 1) * span] = jnp.where(valid, value, 0.0).astype(jnp.bfloat16)
    row = lax.broadcasted_iota(jnp.int32, (CODE_ROWS, span), 0)
    code = jnp.where(row == 0, code_ref[0], code_ref[1])
    out_ref[2 * span :] = code.astype(jnp.float32).astype(jnp.bfloat16)


def choose_kernel(a_ref, b_ref, c_ref, d_ref, mine_ref, other_ref):
    span = mine_ref.shape[1]
    region = lax.axis_index("region")
    partner = region + 1 - 2 * lax.rem(region, 2)
    for out_ref, owner in ((mine_ref, region), (other_ref, partner)):
        for slot in range(2):
            wanted = (owner * 2 + slot).astype(jnp.float32)
            value = None
            for ref in (a_ref, b_ref, c_ref, d_ref):
                for place in range(2):
                    code = ref[2 * span :].astype(jnp.float32)[place : place + 1]
                    hit = jnp.where(code == wanted, 1.0, 0.0).astype(jnp.bfloat16)
                    term = ref[place * span : (place + 1) * span] * hit
                    value = term if value is None else value + term
            out_ref[slot] = value


def join_kernel(a_ref, b_ref, out_ref):
    out_ref[...] = a_ref[...] + b_ref[...]


def local(
    kept_diagonal_tile,
    discard_reciprocal,
    discard_by_kept,
    kept_by_discard,
    adjacent_discard_to_kept,
    adjacent_kept_to_discard,
    adjacent_site_table,
    retained_slots,
    kept_list_length,
    ancestor_site_map,
):
    places, tile_span = retained_slots.shape
    wide, tall = kept_diagonal_tile.shape[1], discard_reciprocal.shape[1]
    params = pltpu.CompilerParams(vmem_limit_bytes=LIMIT)
    small = jax.ShapeDtypeStruct((places, tile_span, tile_span), jnp.bfloat16)

    def block(rows, columns):
        return pl.BlockSpec((1, rows, columns), lambda l: (l, 0, 0))

    own = (retained_slots, kept_diagonal_tile, discard_reciprocal, discard_by_kept, kept_by_discard)

    def self_update(*own):
        return pl.pallas_call(
            self_kernel,
            grid=(places,),
            in_specs=[VMEM, block(wide, wide), block(tall, tall), block(tall, wide), block(wide, tall)],
            out_specs=block(tile_span, tile_span),
            out_shape=jax.ShapeDtypeStruct((places, tile_span, tile_span), jnp.float32),
            compiler_params=params,
            name="self_update",
        )(*own)

    def load(first, sources):
        shapes = [(4,) + v.shape[2:] if v.ndim == 4 else v.shape for v in sources]
        return pl.pallas_call(
            functools.partial(load_kernel, first),
            in_specs=[HBM] * len(sources),
            out_specs=[VMEM] * len(sources),
            out_shape=[pltpu.VMEM(shape, v.dtype) for shape, v in zip(shapes, sources)],
            scratch_shapes=[pltpu.SemaphoreType.DMA((12,))],
            compiler_params=params,
            name="load",
        )(*[pltpu.with_memory_space_constraint(v, pltpu.HBM) for v in sources])

    coupled = (adjacent_kept_to_discard, adjacent_discard_to_kept)
    far_slots = [turn(retained_slots, by) for by in (2, -2)]
    site, inverse, *far_pair = load(2, (adjacent_site_table, discard_reciprocal) + coupled)
    message = jax.ShapeDtypeStruct((places * tile_span + CODE_ROWS, tile_span), jnp.bfloat16)
    far = pl.pallas_call(
        far_kernel,
        in_specs=[VMEM] * 7,
        out_specs=[VMEM] * 2,
        out_shape=[message] * 2,
        compiler_params=params,
        name="far_update",
    )(*far_slots, retained_slots, site, inverse, *far_pair)
    passed = [turn(value, by) for value, by in zip(far, (1, -1))]
    coupled, own, far = lax.optimization_barrier((coupled, own, far))
    near_pair = load(0, coupled)
    sent = pl.pallas_call(
        step_kernel,
        in_specs=[VMEM] * 6,
        out_specs=[VMEM] * 2,
        out_shape=[small, small],
        compiler_params=params,
        name="near_update",
    )(*passed, site, inverse, *near_pair)
    arrived = [turn(sent[0], 1), turn(sent[1], -1)]
    base = self_update(*own)

    child = pl.pallas_call(
        child_kernel,
        in_specs=[SMEM, SMEM] + [VMEM] * 3,
        out_specs=VMEM,
        out_shape=message,
        compiler_params=params,
        name="child",
    )(kept_list_length, ancestor_site_map, base, *arrived)

    gathered = [child] + [shift(child, "region", by) for by in (4, 2, -2)]
    mine, other = pl.pallas_call(
        choose_kernel,
        in_specs=[VMEM] * 4,
        out_specs=[VMEM, VMEM],
        out_shape=[small, small],
        compiler_params=params,
        name="choose",
    )(*gathered)
    partners = [(i, i ^ 1) for i in range(lax.axis_size("region"))]
    received = lax.ppermute(other, "region", partners)
    return pl.pallas_call(
        join_kernel,
        in_specs=[VMEM] * 2,
        out_specs=VMEM,
        out_shape=small,
        compiler_params=params,
        name="join",
    )(mine, received)


def solution(mesh):
    in_specs = (
        P(("region", "box"), None, None),
        P(("region", "box"), None, None),
        P(("region", "box"), None, None),
        P(("region", "box"), None, None),
        P(("region", "box"), None, None, None),
        P(("region", "box"), None, None, None),
        P(("region", "box"), None),
        P(("region", "box"), None),
        P(("region", "box")),
        P(("region", "box")),
    )
    out_specs = P(("region", "box"), None, None)
    return jax.shard_map(local, mesh=mesh, in_specs=in_specs, out_specs=out_specs, check_vma=False)
```

time: 62.1 us -> 55.6 us (0.90)
  the two profiles are of different devices: /device:TPU:1 before, /device:TPU:25 now
where the time goes in v2:
time: 55.6 us
  waiting for transfers between devices  26.5 us (48%)
  starting transfers between devices  15.5 us (28%)
  Pallas kernels  13.5 us (24%)
    ppermute x6, waiting for transfers between devices, turn(): return lax.ppermute(value, ('region', 'box'), pairs)  15 us
    ppermute x3, waiting for transfers between devices, shift(): lax.ppermute(value, axis, [(i, (i + by) % length) for i in range(length)])  10.3 us
    ppermute x6, starting transfers between devices, turn(): return lax.ppermute(value, ('region', 'box'), pairs)  9.29 us
    ppermute x3, starting transfers between devices, shift(): lax.ppermute(value, axis, [(i, (i + by) % length) for i in range(length)])  5.51 us
    pallas_call x2, Pallas kernels, load(): pl.pallas_call(functools.partial(load_kernel, first), in_specs=[HBM] * le...  4.83 us
    pallas_call x1, Pallas kernels, self_update(): pl.pallas_call(self_kernel, grid=(places,), in_specs=[VMEM, block(wide, w...  2.36 us
    pallas_call x1, Pallas kernels, local(): pl.pallas_call(step_kernel, in_specs=[VMEM] * 6, out_specs=[VMEM] * 2, ou...  2.32 us
    pallas_call x1, Pallas kernels, local(): pl.pallas_call(far_kernel, in_specs=[VMEM] * 7, out_specs=[VMEM] * 2, out...  2.27 us
  transfers between devices with their start and end apart: 10, of which 8 were waited for; matrix products, arithmetic and copies ran while one was open for 0% of the time, Pallas kernels for 13%

profile of v2, /device:TPU:25, one launch (start us, length us, event | category | flops | bytes accessed | tf_op | source)
XLA Modules:
  0.0 55.6 jit_solution(12062668764698124311)
XLA Ops:
  0.0 6.2 %collective-permute-start = (s32[2,256]{1,0:T(2,128)}, s32[2,256]{1,0:T(2,128)S(1)}, u32[]{:S(2)}, u32[]{:S(2)}) collective-permute-start(s32[2,256]{1,0:T(2,128)} %slots_ref), channel_id=1, source_target_pairs={{0,2},{1,3},{2,4},{3,5},{4,6},{5,7},{6,8},{7,9},{8,10},{9,11},{10,... | collective-permute-start | bytes 6152 | tf_op jit(solution)/shard_map/ppermute | solution.py:32
  6.2 0.0 collective-permute-start.1
  6.2 2.6 %load.2 = (s32[2,4]{1,0:T(2,128)S(1)}, bf16[2,512,512]{2,1,0:T(8,128)(2,1)S(1)}, bf16[4,512,512]{2,1,0:T(8,128)(2,1)S(1)}, bf16[4,512,512]{2,1,0:T(8,128)(2,1)S(1)}) custom-call(s32[2,4]{1,0:T(2,128)} %refs_0_.1, bf16[2,512,512]{2,1,0:T(8,128)(2,1)} %inverse_ref, bf16[2,4,512,512]{3,2,1,0:T(8,128)(2,1)} %refs_0_.2, bf16[2,4,512,512]{3,2,1,0:T(8,128)(2,1)} %refs_1_.2), custom_call_target="tpu_custom_call" | custom-call | tf_op jit(solution)/shard_map/load/pallas_call | solution.py:219
  8.8 0.0 collective-permute-done.one_ref
  8.8 3.1 %collective-permute-done.1.two_ref = s32[2,256]{1,0:T(2,128)S(1)} collective-permute-done((s32[2,256]{1,0:T(2,128)}, s32[2,256]{1,0:T(2,128)S(1)}, u32[]{:S(2)}, u32[]{:S(2)}) %collective-permute-start.1) | collective-permute-done | bytes 2080 | tf_op jit(solution)/shard_map/ppermute | solution.py:32
  11.9 0.0 copy-done.4
  11.9 2.3 %far_update.1 = (bf16[528,256]{1,0:T(8,128)(2,1)S(1)}, bf16[528,256]{1,0:T(8,128)(2,1)S(1)}) custom-call(s32[2,256]{1,0:T(2,128)S(1)} %collective-permute-done.one_ref, s32[2,256]{1,0:T(2,128)S(1)} %collective-permute-done.1.two_ref, s32[2,256]{1,0:T(2,128)S(1)} %copy-done.4, s32[2,4]{1,0:T(2,128)S(1)} %get-tuple-element.24.site_ref, ...), custom_call_target="tpu_custom_call" | custom-call | tf_op jit(solution)/shard_map/far_update/pallas_call | solution.py:233
  14.1 1.1 %collective-permute-start.2 = (bf16[528,256]{1,0:T(8,128)(2,1)S(1)}, bf16[528,256]{1,0:T(8,128)(2,1)S(1)}, u32[]{:S(2)}, u32[]{:S(2)}) collective-permute-start(bf16[528,256]{1,0:T(8,128)(2,1)S(1)} %get-tuple-element.28), channel_id=1, source_target_pairs={{0,1},{1,2},{2,3},{3,4},{4,5},{5,6},{6,7},{7,8},{8,9},{9,10},{10,1... | collective-permute-start | bytes 811016 | tf_op jit(solution)/shard_map/ppermute | solution.py:32
  15.2 0.5 collective-permute-start.3
  15.7 2.2 %load.3 = (bf16[4,512,512]{2,1,0:T(8,128)(2,1)S(1)}, bf16[4,512,512]{2,1,0:T(8,128)(2,1)S(1)}) custom-call(bf16[2,4,512,512]{3,2,1,0:T(8,128)(2,1)} %refs_0_.2, bf16[2,4,512,512]{3,2,1,0:T(8,128)(2,1)} %refs_1_.2), custom_call_target="tpu_custom_call" | custom-call | tf_op jit(solution)/shard_map/load/pallas_call | solution.py:219
  17.9 3.2 %collective-permute-done.2.one_ref = bf16[528,256]{1,0:T(8,128)(2,1)S(1)} collective-permute-done((bf16[528,256]{1,0:T(8,128)(2,1)S(1)}, bf16[528,256]{1,0:T(8,128)(2,1)S(1)}, u32[]{:S(2)}, u32[]{:S(2)}) %collective-permute-start.2) | collective-permute-done | bytes 270368 | tf_op jit(solution)/shard_map/ppermute | solution.py:32
  21.2 2.2 %collective-permute-done.3.two_ref = bf16[528,256]{1,0:T(8,128)(2,1)S(1)} collective-permute-done((bf16[528,256]{1,0:T(8,128)(2,1)S(1)}, bf16[528,256]{1,0:T(8,128)(2,1)S(1)}, u32[]{:S(2)}, u32[]{:S(2)}) %collective-permute-start.3) | collective-permute-done | bytes 270368 | tf_op jit(solution)/shard_map/ppermute | solution.py:32
  23.4 2.3 %near_update.1 = (bf16[2,256,256]{2,1,0:T(8,128)(2,1)S(1)}, bf16[2,256,256]{2,1,0:T(8,128)(2,1)S(1)}) custom-call(bf16[528,256]{1,0:T(8,128)(2,1)S(1)} %collective-permute-done.2.one_ref, bf16[528,256]{1,0:T(8,128)(2,1)S(1)} %collective-permute-done.3.two_ref, s32[2,4]{1,0:T(2,128)S(1)} %get-tuple-element.24.site_ref, ...), custom_call_target="tpu_custom_call" | custom-call | tf_op jit(solution)/shard_map/near_update/pallas_call | solution.py:244
  25.7 0.9 %collective-permute-start.4 = (bf16[2,256,256]{2,1,0:T(8,128)(2,1)S(1)}, bf16[2,256,256]{2,1,0:T(8,128)(2,1)S(1)}, u32[]{:S(2)}, u32[]{:S(2)}) collective-permute-start(bf16[2,256,256]{2,1,0:T(8,128)(2,1)S(1)} %get-tuple-element.39), channel_id=1, source_target_pairs={{0,1},{1,2},{2,3},{3,4},{4,5},{5,6},{6,7},{7,8},{8,9},{9,10},{10,1... | collective-permute-start | bytes 786440 | tf_op jit(solution)/shard_map/ppermute | solution.py:32
  26.7 0.6 %collective-permute-start.5 = (bf16[2,256,256]{2,1,0:T(8,128)(2,1)S(1)}, bf16[2,256,256]{2,1,0:T(8,128)(2,1)S(1)}, u32[]{:S(2)}, u32[]{:S(2)}) collective-permute-start(bf16[2,256,256]{2,1,0:T(8,128)(2,1)S(1)} %get-tuple-element.40), channel_id=1, source_target_pairs={{0,32},{1,0},{2,1},{3,2},{4,3},{5,4},{6,5},{7,6},{8,7},{9,8},{10,9... | collective-permute-start | bytes 786440 | tf_op jit(solution)/shard_map/ppermute | solution.py:32
  27.3 0.0 copy-done
  27.3 0.0 copy-done.1
  27.3 0.0 copy-done.3
  27.3 2.4 %self_update.1.base_ref = f32[2,256,256]{2,1,0:T(8,128)S(1)} custom-call(s32[2,256]{1,0:T(2,128)S(1)} %copy-done.4, bf16[2,512,512]{2,1,0:T(8,128)(2,1)S(1)} %copy-done.1, bf16[2,512,512]{2,1,0:T(8,128)(2,1)S(1)} %copy-done, bf16[2,512,512]{2,1,0:T(8,128)(2,1)S(1)} %copy-done.2, bf16[2,512,512]{2,1,0:T(8,128)(2,1)S(1)} %copy-done.3), custom_call_target="tpu_custom_call" | custom-call | tf_op jit(solution)/shard_map/self_update/pallas_call | solution.py:207
  29.6 3.2 %collective-permute-done.4.a_ref = bf16[2,256,256]{2,1,0:T(8,128)(2,1)S(1)} collective-permute-done((bf16[2,256,256]{2,1,0:T(8,128)(2,1)S(1)}, bf16[2,256,256]{2,1,0:T(8,128)(2,1)S(1)}, u32[]{:S(2)}, u32[]{:S(2)}) %collective-permute-start.4) | collective-permute-done | bytes 262176 | tf_op jit(solution)/shard_map/ppermute | solution.py:32
  32.9 3.3 %collective-permute-done.5.b_ref = bf16[2,256,256]{2,1,0:T(8,128)(2,1)S(1)} collective-permute-done((bf16[2,256,256]{2,1,0:T(8,128)(2,1)S(1)}, bf16[2,256,256]{2,1,0:T(8,128)(2,1)S(1)}, u32[]{:S(2)}, u32[]{:S(2)}) %collective-permute-start.5) | collective-permute-done | bytes 262176 | tf_op jit(solution)/shard_map/ppermute | solution.py:32
  36.1 0.7 %child.1.a_ref = bf16[528,256]{1,0:T(8,128)(2,1)S(1)} custom-call(s32[2]{0:T(128)S(1)} %copy-done.5, s32[2]{0:T(128)S(1)} %copy-done.6, f32[2,256,256]{2,1,0:T(8,128)S(1)} %self_update.1.base_ref, bf16[2,256,256]{2,1,0:T(8,128)(2,1)S(1)} %collective-permute-done.4.a_ref, bf16[2,256,256]{2,1,0:T(8,128)(2,1)S(1)} %collective-permute-done.5.b_ref), custom_call_target="tpu_custom_call" | custom-call | tf_op jit(solution)/shard_map/child/pallas_call | solution.py:255
  36.8 2.8 %collective-permute-start.6 = (bf16[528,256]{1,0:T(8,128)(2,1)S(1)}, bf16[528,256]{1,0:T(8,128)(2,1)S(1)}, u32[]{:S(2)}, u32[]{:S(2)}) collective-permute-start(bf16[528,256]{1,0:T(8,128)(2,1)S(1)} %child.1.a_ref), channel_id=1, source_target_pairs={{0,128},{32,160},{64,192},{96,224},{128,0},{160,32},{192,64},{224,... | collective-permute-start | bytes 811016 | tf_op jit(solution)/shard_map/ppermute | solution.py:21
  39.7 0.3 collective-permute-start.7
  40.0 2.4 %collective-permute-start.8 = (bf16[528,256]{1,0:T(8,128)(2,1)S(1)}, bf16[528,256]{1,0:T(8,128)(2,1)S(1)}, u32[]{:S(2)}, u32[]{:S(2)}) collective-permute-start(bf16[528,256]{1,0:T(8,128)(2,1)S(1)} %child.1.a_ref), channel_id=1, source_target_pairs={{0,192},{32,224},{64,0},{96,32},{128,64},{160,96},{192,128},{224,1... | collective-permute-start | bytes 811016 | tf_op jit(solution)/shard_map/ppermute | solution.py:21
  42.3 4.2 %collective-permute-done.6.b_ref = bf16[528,256]{1,0:T(8,128)(2,1)S(1)} collective-permute-done((bf16[528,256]{1,0:T(8,128)(2,1)S(1)}, bf16[528,256]{1,0:T(8,128)(2,1)S(1)}, u32[]{:S(2)}, u32[]{:S(2)}) %collective-permute-start.6) | collective-permute-done | bytes 270368 | tf_op jit(solution)/shard_map/ppermute | solution.py:21
  46.5 6.1 %collective-permute-done.7.c_ref = bf16[528,256]{1,0:T(8,128)(2,1)S(1)} collective-permute-done((bf16[528,256]{1,0:T(8,128)(2,1)S(1)}, bf16[528,256]{1,0:T(8,128)(2,1)S(1)}, u32[]{:S(2)}, u32[]{:S(2)}) %collective-permute-start.7) | collective-permute-done | bytes 270368 | tf_op jit(solution)/shard_map/ppermute | solution.py:21
  52.6 0.0 collective-permute-done.8.d_ref
  52.6 0.3 choose.1
  53.0 0.7 %collective-permute-start.9 = (bf16[2,256,256]{2,1,0:T(8,128)(2,1)S(1)}, bf16[2,256,256]{2,1,0:T(8,128)(2,1)S(1)}, u32[]{:S(2)}, u32[]{:S(2)}) collective-permute-start(bf16[2,256,256]{2,1,0:T(8,128)(2,1)S(1)} %get-tuple-element.42), channel_id=1, source_target_pairs={{0,32},{32,0},{64,96},{96,64},{128,160},{160,128},{192,224},{224,1... | collective-permute-start | bytes 786440 | tf_op jit(solution)/shard_map/ppermute | solution.py:274
  53.7 1.2 %collective-permute-done.9.b_ref = bf16[2,256,256]{2,1,0:T(8,128)(2,1)S(1)} collective-permute-done((bf16[2,256,256]{2,1,0:T(8,128)(2,1)S(1)}, bf16[2,256,256]{2,1,0:T(8,128)(2,1)S(1)}, u32[]{:S(2)}, u32[]{:S(2)}) %collective-permute-start.9) | collective-permute-done | bytes 262176 | tf_op jit(solution)/shard_map/ppermute | solution.py:274
  54.8 0.7 %join.1 = bf16[2,256,256]{2,1,0:T(8,128)(2,1)} custom-call(bf16[2,256,256]{2,1,0:T(8,128)(2,1)S(1)} %get-tuple-element.41.a_ref, bf16[2,256,256]{2,1,0:T(8,128)(2,1)S(1)} %collective-permute-done.9.b_ref), custom_call_target="tpu_custom_call" | custom-call | tf_op jit(solution)/shard_map/join/pallas_call | solution.py:275
  (10 shorter events, 0.0 us)
Async XLA Ops:
  0.0 11.9 %copy-start.4 = (s32[2,256]{1,0:T(2,128)S(1)}, s32[2,256]{1,0:T(2,128)}, u32[]{:S(2)}) copy-start(s32[2,256]{1,0:T(2,128)} %slots_ref) | copy-start | bytes 6148
  0.0 8.8 %collective-permute-start = (s32[2,256]{1,0:T(2,128)}, s32[2,256]{1,0:T(2,128)S(1)}, u32[]{:S(2)}, u32[]{:S(2)}) collective-permute-start(s32[2,256]{1,0:T(2,128)} %slots_ref), channel_id=1, source_target_pairs={{0,2},{1,3},{2,4},{3,5},{4,6},{5,7},{6,8},{7,9},{8,10},{9,11},{10,... | collective-permute-start | bytes 6152 | tf_op jit(solution)/shard_map/ppermute | solution.py:32
  6.2 5.7 %collective-permute-start.1 = (s32[2,256]{1,0:T(2,128)}, s32[2,256]{1,0:T(2,128)S(1)}, u32[]{:S(2)}, u32[]{:S(2)}) collective-permute-start(s32[2,256]{1,0:T(2,128)} %slots_ref), channel_id=1, source_target_pairs={{0,32},{1,33},{2,0},{3,1},{4,2},{5,3},{6,4},{7,5},{8,6},{9,7},{10,... | collective-permute-start | bytes 6152 | tf_op jit(solution)/shard_map/ppermute | solution.py:32
  14.1 7.0 %collective-permute-start.2 = (bf16[528,256]{1,0:T(8,128)(2,1)S(1)}, bf16[528,256]{1,0:T(8,128)(2,1)S(1)}, u32[]{:S(2)}, u32[]{:S(2)}) collective-permute-start(bf16[528,256]{1,0:T(8,128)(2,1)S(1)} %get-tuple-element.28), channel_id=1, source_target_pairs={{0,1},{1,2},{2,3},{3,4},{4,5},{5,6},{6,7},{7,8},{8,9},{9,10},{10,1... | collective-permute-start | bytes 811016 | tf_op jit(solution)/shard_map/ppermute | solution.py:32
  15.2 8.2 %collective-permute-start.3 = (bf16[528,256]{1,0:T(8,128)(2,1)S(1)}, bf16[528,256]{1,0:T(8,128)(2,1)S(1)}, u32[]{:S(2)}, u32[]{:S(2)}) collective-permute-start(bf16[528,256]{1,0:T(8,128)(2,1)S(1)} %get-tuple-element.29), channel_id=1, source_target_pairs={{0,32},{1,0},{2,1},{3,2},{4,3},{5,4},{6,5},{7,6},{8,7},{9,8},{10,9... | collective-permute-start | bytes 811016 | tf_op jit(solution)/shard_map/ppermute | solution.py:32
  23.4 3.9 %copy-start = (bf16[2,512,512]{2,1,0:T(8,128)(2,1)S(1)}, bf16[2,512,512]{2,1,0:T(8,128)(2,1)}, u32[]{:S(2)}) copy-start(bf16[2,512,512]{2,1,0:T(8,128)(2,1)} %inverse_ref) | copy-start | bytes 3145732
  23.4 3.9 %copy-start.1 = (bf16[2,512,512]{2,1,0:T(8,128)(2,1)S(1)}, bf16[2,512,512]{2,1,0:T(8,128)(2,1)}, u32[]{:S(2)}) copy-start(bf16[2,512,512]{2,1,0:T(8,128)(2,1)} %tile_ref) | copy-start | bytes 3145732
  23.4 3.9 %copy-start.2 = (bf16[2,512,512]{2,1,0:T(8,128)(2,1)S(1)}, bf16[2,512,512]{2,1,0:T(8,128)(2,1)}, u32[]{:S(2)}) copy-start(bf16[2,512,512]{2,1,0:T(8,128)(2,1)} %by_kept_ref) | copy-start | bytes 3145732
  23.4 3.9 %copy-start.3 = (bf16[2,512,512]{2,1,0:T(8,128)(2,1)S(1)}, bf16[2,512,512]{2,1,0:T(8,128)(2,1)}, u32[]{:S(2)}) copy-start(bf16[2,512,512]{2,1,0:T(8,128)(2,1)} %by_discard_ref) | copy-start | bytes 3145732
  25.7 7.2 %collective-permute-start.4 = (bf16[2,256,256]{2,1,0:T(8,128)(2,1)S(1)}, bf16[2,256,256]{2,1,0:T(8,128)(2,1)S(1)}, u32[]{:S(2)}, u32[]{:S(2)}) collective-permute-start(bf16[2,256,256]{2,1,0:T(8,128)(2,1)S(1)} %get-tuple-element.39), channel_id=1, source_target_pairs={{0,1},{1,2},{2,3},{3,4},{4,5},{5,6},{6,7},{7,8},{8,9},{9,10},{10,1... | collective-permute-start | bytes 786440 | tf_op jit(solution)/shard_map/ppermute | solution.py:32
  26.6 9.5 %copy-start.5 = (s32[2]{0:T(128)S(1)}, s32[2]{0:T(128)}, u32[]{:S(2)}) copy-start(s32[2]{0:T(128)} %length_ref.1) | copy-start | bytes 28
  26.7 9.5 %copy-start.6 = (s32[2]{0:T(128)S(1)}, s32[2]{0:T(128)}, u32[]{:S(2)}) copy-start(s32[2]{0:T(128)} %code_ref.1) | copy-start | bytes 28
  26.7 9.5 %collective-permute-start.5 = (bf16[2,256,256]{2,1,0:T(8,128)(2,1)S(1)}, bf16[2,256,256]{2,1,0:T(8,128)(2,1)S(1)}, u32[]{:S(2)}, u32[]{:S(2)}) collective-permute-start(bf16[2,256,256]{2,1,0:T(8,128)(2,1)S(1)} %get-tuple-element.40), channel_id=1, source_target_pairs={{0,32},{1,0},{2,1},{3,2},{4,3},{5,4},{6,5},{7,6},{8,7},{9,8},{10,9... | collective-permute-start | bytes 786440 | tf_op jit(solution)/shard_map/ppermute | solution.py:32
  36.8 9.7 %collective-permute-start.6 = (bf16[528,256]{1,0:T(8,128)(2,1)S(1)}, bf16[528,256]{1,0:T(8,128)(2,1)S(1)}, u32[]{:S(2)}, u32[]{:S(2)}) collective-permute-start(bf16[528,256]{1,0:T(8,128)(2,1)S(1)} %child.1.a_ref), channel_id=1, source_target_pairs={{0,128},{32,160},{64,192},{96,224},{128,0},{160,32},{192,64},{224,... | collective-permute-start | bytes 811016 | tf_op jit(solution)/shard_map/ppermute | solution.py:21
  39.7 13.0 %collective-permute-start.7 = (bf16[528,256]{1,0:T(8,128)(2,1)S(1)}, bf16[528,256]{1,0:T(8,128)(2,1)S(1)}, u32[]{:S(2)}, u32[]{:S(2)}) collective-permute-start(bf16[528,256]{1,0:T(8,128)(2,1)S(1)} %child.1.a_ref), channel_id=1, source_target_pairs={{0,64},{32,96},{64,128},{96,160},{128,192},{160,224},{192,0},{224,... | collective-permute-start | bytes 811016 | tf_op jit(solution)/shard_map/ppermute | solution.py:21
  40.0 12.7 %collective-permute-start.8 = (bf16[528,256]{1,0:T(8,128)(2,1)S(1)}, bf16[528,256]{1,0:T(8,128)(2,1)S(1)}, u32[]{:S(2)}, u32[]{:S(2)}) collective-permute-start(bf16[528,256]{1,0:T(8,128)(2,1)S(1)} %child.1.a_ref), channel_id=1, source_target_pairs={{0,192},{32,224},{64,0},{96,32},{128,64},{160,96},{192,128},{224,1... | collective-permute-start | bytes 811016 | tf_op jit(solution)/shard_map/ppermute | solution.py:21
  53.0 1.8 %collective-permute-start.9 = (bf16[2,256,256]{2,1,0:T(8,128)(2,1)S(1)}, bf16[2,256,256]{2,1,0:T(8,128)(2,1)S(1)}, u32[]{:S(2)}, u32[]{:S(2)}) collective-permute-start(bf16[2,256,256]{2,1,0:T(8,128)(2,1)S(1)} %get-tuple-element.42), channel_id=1, source_target_pairs={{0,32},{32,0},{64,96},{96,64},{128,160},{160,128},{192,224},{224,1... | collective-permute-start | bytes 786440 | tf_op jit(solution)/shard_map/ppermute | solution.py:274

commit v3 on v2

--- a/solution.py
+++ b/solution.py
@@ -68,54 +68,93 @@
     count = (len(refs) - 1) // 2
     sources, outs, sems = refs[:count], refs[count : 2 * count], refs[2 * count]
     copies = []
-
-    def copy(source, out):
-        copies.append(pltpu.make_async_copy(source, out, sems.at[len(copies)]))
-
-    along = directions()
     for source, out in zip(sources, outs):
-        if len(source.shape) == 4:
-            for which in range(2):
-                for place in range(2):
-                    copy(source.at[place, first + along[which]], out.at[2 * which + place])
-        else:
-            copy(source, out)
+        for piece, target in pieces(first, source, out):
+            copies.append(pltpu.make_async_copy(piece, target, sems.at[len(copies)]))
     for each in copies:
         each.start()
     for each in copies:
         each.wait()
 
 
-def near_kernel(first, span, slots_of, site_ref, inverse, right, left):
+def pieces(first, source, out):
+    if len(source.shape) != 4:
+        return [(source, out)]
     along = directions()
-    core = along[0]
+    return [
+        (source.at[place, first + along[which]], out.at[2 * which + place])
+        for which in range(2)
+        for place in range(2)
+    ]
+
+
+def reduce_kernel(
+    first, table_ref, inverse_ref, right_ref, left_ref, site, inverse, reduced, left, right, sems
+):
+    early, late = [], []
+    for group, source, out in (
+        (early, right_ref, right),
+        (early, inverse_ref, inverse),
+        (late, left_ref, left),
+        (late, table_ref, site),
+    ):
+        for piece, target in pieces(first, source, out):
+            group.append(pltpu.make_async_copy(piece, target, sems.at[len(early) + len(late)]))
+    for each in early + late:
+        each.start()
+    for each in early:
+        each.wait()
+    for at in range(4):
+        reduced[at] = dot(inverse[at % 2], right[at]).astype(jnp.bfloat16)
+    for each in late:
+        each.wait()
+
+
+def targets_of(first, site_ref):
+    along = directions()
     position = lax.axis_index("box")
-    pairs = [(which, place) for which in range(2) for place in range(2)]
-    targets, columns, rows = [], [], []
-    for which, place in pairs:
+    targets = []
+    for which in range(2):
         there = position + offsets_list[first] * (1 - 2 * along[which])
         inside = (there >= 0) & (there < lax.axis_size("box"))
-        one, two = (site_ref[place : place + 1, first + i : first + i + 1] for i in (which, 1 - which))
-        target = jnp.where(inside, jnp.where(core == 0, one, two), 2)
-        slots = slots_of(which)
-        column, row = pickers(jnp.where(target == 0, slots[0:1], slots[1:2]), span)
-        targets.append(target)
-        columns.append(column)
-        rows.append(row)
-    picked = [dot(right[at], columns[at]).astype(jnp.bfloat16) for at in range(4)]
-    reduced = [dot(inverse[place], picked[at]).astype(jnp.bfloat16) for at, (_, place) in enumerate(pairs)]
-    coupled = [dot(rows[at], left[at]).astype(jnp.bfloat16) for at in range(4)]
-    near = [dot(coupled[at], reduced[at]) for at in range(4)]
+        row = []
+        for place in range(2):
+            one, two = (site_ref[place : place + 1, first + i : first + i + 1] for i in (which, 1 - which))
+            row.append(jnp.where(inside, jnp.where(along[0] == 0, one, two), 2))
+        targets.append(row)
+    return targets
+
+
+def join_places(targets, near):
     return [
-        [sum(jnp.where(targets[2 * which + p] == t, near[2 * which + p], 0.0) for p in range(2)) for t in range(2)]
-        for which in range(2)
+        [sum(jnp.where(targets[w][p] == t, near[2 * w + p], 0.0) for p in range(2)) for t in range(2)]
+        for w in range(2)
     ]
 
 
-def far_kernel(one_ref, two_ref, own_ref, site_ref, inverse, right, left, out_one, out_two):
+def whole_kernel(site_ref, inverse, right, left, out):
+    reduced = [dot(inverse[at % 2], right[at]).astype(jnp.bfloat16) for at in range(4)]
+    near = [dot(left[at], reduced[at]) for at in range(4)]
+    sums = join_places(targets_of(0, site_ref), near)
+    for which in range(2):
+        for t in range(2):
+            out[2 * which + t] = sums[which][t].astype(jnp.bfloat16)
+
+
+def far_kernel(one_ref, two_ref, own_ref, site_ref, reduced, left, out_one, out_two):
     span = own_ref.shape[1]
-    from_there = (two_ref, one_ref)
-    updates = near_kernel(2, left.shape[1], lambda w: from_there[w][...], site_ref, inverse, right, left)
+    from_there = (two_ref[...], one_ref[...])
+    targets = targets_of(2, site_ref)
+    picks = []
+    for which in range(2):
+        slots = from_there[which]
+        for place in range(2):
+            own_slots = jnp.where(targets[which][place] == 0, slots[0:1], slots[1:2])
+            picks.append(pickers(own_slots, left.shape[1]))
+    picked = [dot(reduced[at], picks[at][0]).astype(jnp.bfloat16) for at in range(4)]
+    coupled = [dot(picks[at][1], left[at]).astype(jnp.bfloat16) for at in range(4)]
+    near = [dot(coupled[at], picked[at]) for at in range(4)]
+    updates = join_places(targets, near)
     own = own_ref[...]
     row = lax.broadcasted_iota(jnp.int32, (CODE_ROWS, span), 0)
     halves = (own >> 1, own & 1)
@@ -129,50 +168,51 @@
         out[2 * span :] = code
 
 
-def step_kernel(one_ref, two_ref, site_ref, inverse, right, left, out_one, out_two):
+def step_kernel(one_ref, two_ref, near_ref, out_one, out_two):
     span = out_one.shape[1]
     passed = (one_ref, two_ref)
-
-    def slots_of(which):
+    picks = []
+    for which in range(2):
         code = passed[1 - which][2 * span :].astype(jnp.float32).astype(jnp.int32)
-        return code[0:2] * 2 + code[2:4]
-
-    updates = near_kernel(0, left.shape[1], slots_of, site_ref, inverse, right, left)
+        slots = code[0:2] * 2 + code[2:4]
+        picks += [pickers(slots[t : t + 1], near_ref.shape[1]) for t in range(2)]
+    half = [dot(near_ref[at], picks[at][0]).astype(jnp.bfloat16) for at in range(4)]
+    near = [dot(picks[at][1], half[at]) for at in range(4)]
     for which, out in enumerate((out_one, out_two)):
         for t in range(2):
             far = passed[which][t * span : (t + 1) * span].astype(jnp.float32)
-            out[t] = (updates[which][t] + far).astype(jnp.bfloat16)
-
-
-def child_kernel(length_ref, code_ref, base_ref, a_ref, b_ref, out_ref):
-    span = base_ref.shape[1]
-    for place in range(base_ref.shape[0]):
-        value = base_ref[place]
-        for ref in (a_ref, b_ref):
-            value = value - ref[place].astype(jnp.float32)
+            out[t] = (near[2 * which + t] + far).astype(jnp.bfloat16)
+
+
+def child_kernel(length_ref, code_ref, base_ref, one_ref, two_ref, *outs):
+    places, span = base_ref.shape[:2]
+    row = lax.broadcasted_iota(jnp.int32, (span, span), 0)
+    column = lax.broadcasted_iota(jnp.int32, (span, span), 1)
+    for place in range(places):
+        value = base_ref[place] - one_ref[place].astype(jnp.float32) - two_ref[place].astype(jnp.float32)
         length = length_ref[place]
-        row = lax.broadcasted_iota(jnp.int32, (span, span), 0)
-        column = lax.broadcasted_iota(jnp.int32, (span, span), 1)
         valid = (row < length) & (column < length)
-        out_ref[place * span : (place + 1) * span] = jnp.where(valid, value, 0.0).astype(jnp.bfloat16)
+        outs[place][0:span] = jnp.where(valid, value, 0.0).astype(jnp.bfloat16)
     row = lax.broadcasted_iota(jnp.int32, (CODE_ROWS, span), 0)
     code = jnp.where(row == 0, code_ref[0], code_ref[1])
-    out_ref[2 * span :] = code.astype(jnp.float32).astype(jnp.bfloat16)
-
-
-def choose_kernel(a_ref, b_ref, c_ref, d_ref, mine_ref, other_ref):
+    outs[0][span:] = code.astype(jnp.float32).astype(jnp.bfloat16)
+
+
+def choose_kernel(*refs):
+    sources, (mine_ref, other_ref) = refs[:-2], refs[-2:]
+    children = (sources[: len(sources) // 2], sources[len(sources) // 2 :])
     span = mine_ref.shape[1]
     region = lax.axis_index("region")
     partner = region + 1 - 2 * lax.rem(region, 2)
+    codes = [ref[span:].astype(jnp.float32) for ref in children[0]]
     for out_ref, owner in ((mine_ref, region), (other_ref, partner)):
         for slot in range(2):
             wanted = (owner * 2 + slot).astype(jnp.float32)
             value = None
-            for ref in (a_ref, b_ref, c_ref, d_ref):
-                for place in range(2):
-                    code = ref[2 * span :].astype(jnp.float32)[place : place + 1]
-                    hit = jnp.where(code == wanted, 1.0, 0.0).astype(jnp.bfloat16)
-                    term = ref[place * span : (place + 1) * span] * hit
+            for place in range(2):
+                for ref, code in zip(children[place], codes):
+                    hit = jnp.where(code[place : place + 1] == wanted, 1.0, 0.0).astype(jnp.bfloat16)
+                    term = ref[0:span] * hit
                     value = term if value is None else value + term
             out_ref[slot] = value
 
@@ -221,50 +261,78 @@
             in_specs=[HBM] * len(sources),
             out_specs=[VMEM] * len(sources),
             out_shape=[pltpu.VMEM(shape, v.dtype) for shape, v in zip(shapes, sources)],
-            scratch_shapes=[pltpu.SemaphoreType.DMA((12,))],
+            scratch_shapes=[pltpu.SemaphoreType.DMA((8,))],
             compiler_params=params,
             name="load",
         )(*[pltpu.with_memory_space_constraint(v, pltpu.HBM) for v in sources])
 
     coupled = (adjacent_kept_to_discard, adjacent_discard_to_kept)
     far_slots = [turn(retained_slots, by) for by in (2, -2)]
-    site, inverse, *far_pair = load(2, (adjacent_site_table, discard_reciprocal) + coupled)
+    far_sources = (adjacent_site_table, discard_reciprocal) + coupled
+    rights, lefts = (4, tall, wide), (4, wide, tall)
+    site, inverse, reduced, far_left = pl.pallas_call(
+        functools.partial(reduce_kernel, 2),
+        in_specs=[HBM] * 4,
+        out_specs=[VMEM] * 4,
+        out_shape=[
+            pltpu.VMEM(adjacent_site_table.shape, jnp.int32),
+            pltpu.VMEM(discard_reciprocal.shape, jnp.bfloat16),
+            pltpu.VMEM(rights, jnp.bfloat16),
+            pltpu.VMEM(lefts, jnp.bfloat16),
+        ],
+        scratch_shapes=[pltpu.VMEM(rights, jnp.bfloat16), pltpu.SemaphoreType.DMA((10,))],
+        compiler_params=params,
+        name="load_reduce",
+    )(*[pltpu.with_memory_space_constraint(v, pltpu.HBM) for v in far_sources])
     message = jax.ShapeDtypeStruct((places * tile_span + CODE_ROWS, tile_span), jnp.bfloat16)
     far = pl.pallas_call(
         far_kernel,
-        in_specs=[VMEM] * 7,
+        in_specs=[VMEM] * 6,
         out_specs=[VMEM] * 2,
         out_shape=[message] * 2,
         compiler_params=params,
         name="far_update",
-    )(*far_slots, retained_slots, site, inverse, *far_pair)
+    )(*far_slots, retained_slots, site, reduced, far_left)
     passed = [turn(value, by) for value, by in zip(far, (1, -1))]
     coupled, own, far = lax.optimization_barrier((coupled, own, far))
     near_pair = load(0, coupled)
+    whole = pl.pallas_call(
+        whole_kernel,
+        in_specs=[VMEM] * 4,
+        out_specs=VMEM,
+        out_shape=jax.ShapeDtypeStruct((4, wide, wide), jnp.bfloat16),
+        compiler_params=params,
+        name="whole_update",
+    )(site, inverse, *near_pair)
     sent = pl.pallas_call(
         step_kernel,
-        in_specs=[VMEM] * 6,
+        in_specs=[VMEM] * 3,
         out_specs=[VMEM] * 2,
         out_shape=[small, small],
         compiler_params=params,
         name="near_update",
-    )(*passed, site, inverse, *near_pair)
+    )(*passed, whole)
     arrived = [turn(sent[0], 1), turn(sent[1], -1)]
     base = self_update(*own)
 
-    child = pl.pallas_call(
+    half = jax.ShapeDtypeStruct((tile_span, tile_span), jnp.bfloat16)
+    coded = jax.ShapeDtypeStruct((tile_span + CODE_ROWS, tile_span), jnp.bfloat16)
+    one, two = pl.pallas_call(
         child_kernel,
         in_specs=[SMEM, SMEM] + [VMEM] * 3,
-        out_specs=VMEM,
-        out_shape=message,
+        out_specs=[VMEM] * 2,
+        out_shape=[coded, half],
         compiler_params=params,
         name="child",
     )(kept_list_length, ancestor_site_map, base, *arrived)
 
-    gathered = [child] + [shift(child, "region", by) for by in (4, 2, -2)]
+    one_back, two_ahead = shift(one, "region", 2), shift(two, "region", -2)
+    two_back, one_ahead = shift(two, "region", 2), shift(one, "region", -2)
+    one_far, two_far = shift(one_back, "region", 2), shift(two_ahead, "region", -2)
+    gathered = [one, one_back, one_ahead, one_far, two, two_back, two_ahead, two_far]
     mine, other = pl.pallas_call(
         choose_kernel,
-        in_specs=[VMEM] * 4,
+        in_specs=[VMEM] * 8,
         out_specs=[VMEM, VMEM],
         out_shape=[small, small],
         compiler_params=params,

time: 55.6 us -> 53.7 us (0.966)
  waiting for transfers between devices: 26.5 us -> 20.6 us
  starting transfers between devices: 15.5 us -> 18 us
  Pallas kernels: 13.5 us -> 14.9 us
    pallas_call x3 -> x5, Pallas kernels: 4.91 us -> 8.9 us  [the longest x1 3.22 us: local(): pl.pallas_call(functools.partial(reduce_kernel, 2), in_specs=[HBM] * 4, o...]
    ppermute x6, waiting for transfers between devices: 15 us -> 11.5 us  [turn(): return lax.ppermute(value, ('region', 'box'), pairs)]
    pallas_call x2 -> x1, Pallas kernels: 4.83 us -> 2.21 us  [load(): pl.pallas_call(functools.partial(load_kernel, first), in_specs=[HBM] * le...]
    ppermute x3 -> x6, waiting for transfers between devices: 10.3 us -> 7.88 us  [shift(): lax.ppermute(value, axis, [(i, (i + by) % length) for i in range(length)])]
    ppermute x3 -> x6, starting transfers between devices: 5.51 us -> 7.33 us  [shift(): lax.ppermute(value, axis, [(i, (i + by) % length) for i in range(length)])]
  transfers between devices with their start and end apart: 10 -> 13, of which waited for: 8 -> 8; matrix products, arithmetic and copies ran while one was open for 0% -> 0% of each run, Pallas kernels for 13% -> 19%
where the time goes in v3:
time: 53.7 us
  waiting for transfers between devices  20.6 us (38%)
  starting transfers between devices  18 us (34%)
  Pallas kernels  14.9 us (28%)
    ppermute x6, waiting for transfers between devices, turn(): return lax.ppermute(value, ('region', 'box'), pairs)  11.5 us
    ppermute x6, starting transfers between devices, turn(): return lax.ppermute(value, ('region', 'box'), pairs)  9.47 us
    ppermute x6, waiting for transfers between devices, shift(): lax.ppermute(value, axis, [(i, (i + by) % length) for i in range(length)])  7.88 us
    ppermute x6, starting transfers between devices, shift(): lax.ppermute(value, axis, [(i, (i + by) % length) for i in range(length)])  7.33 us
    pallas_call x1, Pallas kernels, local(): pl.pallas_call(functools.partial(reduce_kernel, 2), in_specs=[HBM] * 4, o...  3.22 us
    pallas_call x1, Pallas kernels, local(): pl.pallas_call(whole_kernel, in_specs=[VMEM] * 4, out_specs=VMEM, out_sha...  2.59 us
    pallas_call x1, Pallas kernels, self_update(): pl.pallas_call(self_kernel, grid=(places,), in_specs=[VMEM, block(wide, w...  2.36 us
    pallas_call x1, Pallas kernels, load(): pl.pallas_call(functools.partial(load_kernel, first), in_specs=[HBM] * le...  2.21 us
  transfers between devices with their start and end apart: 13, of which 8 were waited for; matrix products, arithmetic and copies ran while one was open for 0% of the time, Pallas kernels for 19%

profile of v3, /device:TPU:25, one launch (start us, length us, event | category | flops | bytes accessed | tf_op | source)
XLA Modules:
  0.0 53.7 jit_solution(8972767425000476271)
XLA Ops:
  0.0 6.2 %collective-permute-start = (s32[2,256]{1,0:T(2,128)}, s32[2,256]{1,0:T(2,128)S(1)}, u32[]{:S(2)}, u32[]{:S(2)}) collective-permute-start(s32[2,256]{1,0:T(2,128)} %slots_ref), channel_id=1, source_target_pairs={{0,2},{1,3},{2,4},{3,5},{4,6},{5,7},{6,8},{7,9},{8,10},{9,11},{10,... | collective-permute-start | bytes 6152 | tf_op jit(solution)/shard_map/ppermute | solution.py:32
  6.2 0.0 collective-permute-start.1
  6.2 3.2 %load_reduce.1 = (s32[2,4]{1,0:T(2,128)S(1)}, bf16[2,512,512]{2,1,0:T(8,128)(2,1)S(1)}, bf16[4,512,512]{2,1,0:T(8,128)(2,1)S(1)}, bf16[4,512,512]{2,1,0:T(8,128)(2,1)S(1)}) custom-call(s32[2,4]{1,0:T(2,128)} %table_ref.1, bf16[2,512,512]{2,1,0:T(8,128)(2,1)} %inverse_ref.2, bf16[2,4,512,512]{3,2,1,0:T(8,128)(2,1)} %refs_0_, bf16[2,4,512,512]{3,2,1,0:T(8,128)(2,1)} %refs_1_), custom_call_target="tpu_custom_call" | custom-call | tf_op jit(solution)/shard_map/load_reduce/pallas_call | solution.py:273
  9.4 2.4 %collective-permute-done.1.two_ref = s32[2,256]{1,0:T(2,128)S(1)} collective-permute-done((s32[2,256]{1,0:T(2,128)}, s32[2,256]{1,0:T(2,128)S(1)}, u32[]{:S(2)}, u32[]{:S(2)}) %collective-permute-start.1) | collective-permute-done | bytes 2080 | tf_op jit(solution)/shard_map/ppermute | solution.py:32
  11.9 1.7 %far_update.1 = (bf16[528,256]{1,0:T(8,128)(2,1)S(1)}, bf16[528,256]{1,0:T(8,128)(2,1)S(1)}) custom-call(s32[2,256]{1,0:T(2,128)S(1)} %collective-permute-done.one_ref, s32[2,256]{1,0:T(2,128)S(1)} %collective-permute-done.1.two_ref, s32[2,256]{1,0:T(2,128)S(1)} %copy-done.4, s32[2,4]{1,0:T(2,128)S(1)} %get-tuple-element.26.site_ref, ...), custom_call_target="tpu_custom_call" | custom-call | tf_op jit(solution)/shard_map/far_update/pallas_call | solution.py:288
  13.6 1.7 %collective-permute-start.2 = (bf16[528,256]{1,0:T(8,128)(2,1)S(1)}, bf16[528,256]{1,0:T(8,128)(2,1)S(1)}, u32[]{:S(2)}, u32[]{:S(2)}) collective-permute-start(bf16[528,256]{1,0:T(8,128)(2,1)S(1)} %get-tuple-element.29), channel_id=1, source_target_pairs={{0,1},{1,2},{2,3},{3,4},{4,5},{5,6},{6,7},{7,8},{8,9},{9,10},{10,1... | collective-permute-start | bytes 811016 | tf_op jit(solution)/shard_map/ppermute | solution.py:32
  15.3 2.2 %load.1 = (bf16[4,512,512]{2,1,0:T(8,128)(2,1)S(1)}, bf16[4,512,512]{2,1,0:T(8,128)(2,1)S(1)}) custom-call(bf16[2,4,512,512]{3,2,1,0:T(8,128)(2,1)} %refs_0_, bf16[2,4,512,512]{3,2,1,0:T(8,128)(2,1)} %refs_1_), custom_call_target="tpu_custom_call" | custom-call | tf_op jit(solution)/shard_map/load/pallas_call | solution.py:259
  17.5 0.0 copy-start.2
  17.5 0.0 copy-start.3
  17.5 2.6 %whole_update.1.near_ref = bf16[4,512,512]{2,1,0:T(8,128)(2,1)S(1)} custom-call(s32[2,4]{1,0:T(2,128)S(1)} %get-tuple-element.26.site_ref, bf16[2,512,512]{2,1,0:T(8,128)(2,1)S(1)} %get-tuple-element.36.inverse, bf16[4,512,512]{2,1,0:T(8,128)(2,1)S(1)} %get-tuple-element.39.right, bf16[4,512,512]{2,1,0:T(8,128)(2,1)S(1)} %get-tuple-element.40.left), custom_call_target="tpu_custom_call" | custom-call | tf_op jit(solution)/shard_map/whole_update/pallas_call | solution.py:299
  20.1 0.0 copy-start
  20.1 0.0 copy-start.1
  20.1 0.5 collective-permute-done.2.one_ref
  20.6 2.5 %collective-permute-done.3.two_ref = bf16[528,256]{1,0:T(8,128)(2,1)S(1)} collective-permute-done((bf16[528,256]{1,0:T(8,128)(2,1)S(1)}, bf16[528,256]{1,0:T(8,128)(2,1)S(1)}, u32[]{:S(2)}, u32[]{:S(2)}) %collective-permute-start.3) | collective-permute-done | bytes 270368 | tf_op jit(solution)/shard_map/ppermute | solution.py:32
  23.1 1.1 %near_update.1 = (bf16[2,256,256]{2,1,0:T(8,128)(2,1)S(1)}, bf16[2,256,256]{2,1,0:T(8,128)(2,1)S(1)}) custom-call(bf16[528,256]{1,0:T(8,128)(2,1)S(1)} %collective-permute-done.2.one_ref, bf16[528,256]{1,0:T(8,128)(2,1)S(1)} %collective-permute-done.3.two_ref, bf16[4,512,512]{2,1,0:T(8,128)(2,1)S(1)} %whole_update.1.near_ref), custom_call_target="tpu_custom_call" | custom-call | tf_op jit(solution)/shard_map/near_update/pallas_call | solution.py:307
  24.1 1.6 %collective-permute-start.4 = (bf16[2,256,256]{2,1,0:T(8,128)(2,1)S(1)}, bf16[2,256,256]{2,1,0:T(8,128)(2,1)S(1)}, u32[]{:S(2)}, u32[]{:S(2)}) collective-permute-start(bf16[2,256,256]{2,1,0:T(8,128)(2,1)S(1)} %get-tuple-element.41), channel_id=1, source_target_pairs={{0,1},{1,2},{2,3},{3,4},{4,5},{5,6},{6,7},{7,8},{8,9},{9,10},{10,1... | collective-permute-start | bytes 786440 | tf_op jit(solution)/shard_map/ppermute | solution.py:32
  25.7 2.4 %self_update.1.base_ref = f32[2,256,256]{2,1,0:T(8,128)S(1)} custom-call(s32[2,256]{1,0:T(2,128)S(1)} %copy-done.4, bf16[2,512,512]{2,1,0:T(8,128)(2,1)S(1)} %copy-done.1, bf16[2,512,512]{2,1,0:T(8,128)(2,1)S(1)} %copy-done, bf16[2,512,512]{2,1,0:T(8,128)(2,1)S(1)} %copy-done.2, bf16[2,512,512]{2,1,0:T(8,128)(2,1)S(1)} %copy-done.3), custom_call_target="tpu_custom_call" | custom-call | tf_op jit(solution)/shard_map/self_update/pallas_call | solution.py:247
  28.1 3.5 %collective-permute-done.4.one_ref = bf16[2,256,256]{2,1,0:T(8,128)(2,1)S(1)} collective-permute-done((bf16[2,256,256]{2,1,0:T(8,128)(2,1)S(1)}, bf16[2,256,256]{2,1,0:T(8,128)(2,1)S(1)}, u32[]{:S(2)}, u32[]{:S(2)}) %collective-permute-start.4) | collective-permute-done | bytes 262176 | tf_op jit(solution)/shard_map/ppermute | solution.py:32
  31.6 2.7 %collective-permute-done.5.two_ref = bf16[2,256,256]{2,1,0:T(8,128)(2,1)S(1)} collective-permute-done((bf16[2,256,256]{2,1,0:T(8,128)(2,1)S(1)}, bf16[2,256,256]{2,1,0:T(8,128)(2,1)S(1)}, u32[]{:S(2)}, u32[]{:S(2)}) %collective-permute-start.5) | collective-permute-done | bytes 262176 | tf_op jit(solution)/shard_map/ppermute | solution.py:32
  34.3 0.7 %child.1 = (bf16[272,256]{1,0:T(8,128)(2,1)S(1)}, bf16[256,256]{1,0:T(8,128)(2,1)S(1)}) custom-call(s32[2]{0:T(128)S(1)} %copy-done.5, s32[2]{0:T(128)S(1)} %copy-done.6, f32[2,256,256]{2,1,0:T(8,128)S(1)} %self_update.1.base_ref, bf16[2,256,256]{2,1,0:T(8,128)(2,1)S(1)} %collective-permute-done.4.one_ref, ...), custom_call_target="tpu_custom_call" | custom-call | tf_op jit(solution)/shard_map/child/pallas_call | solution.py:320
  35.0 1.3 %collective-permute-start.6 = (bf16[272,256]{1,0:T(8,128)(2,1)S(1)}, bf16[272,256]{1,0:T(8,128)(2,1)S(1)}, u32[]{:S(2)}, u32[]{:S(2)}) collective-permute-start(bf16[272,256]{1,0:T(8,128)(2,1)S(1)} %get-tuple-element.43.refs_0_), channel_id=1, source_target_pairs={{0,64},{32,96},{64,128},{96,160},{128,192},{160,224},{192,0},{224,... | collective-permute-start | bytes 417800 | tf_op jit(solution)/shard_map/ppermute | solution.py:21
  36.3 1.5 %collective-permute-start.10 = (bf16[256,256]{1,0:T(8,128)(2,1)S(1)}, bf16[256,256]{1,0:T(8,128)(2,1)S(1)}, u32[]{:S(2)}, u32[]{:S(2)}) collective-permute-start(bf16[256,256]{1,0:T(8,128)(2,1)S(1)} %get-tuple-element.44.refs_4_), channel_id=1, source_target_pairs={{0,192},{32,224},{64,0},{96,32},{128,64},{160,96},{192,128},{224,1... | collective-permute-start | bytes 393224 | tf_op jit(solution)/shard_map/ppermute | solution.py:21
  37.8 1.2 %collective-permute-start.7 = (bf16[272,256]{1,0:T(8,128)(2,1)S(1)}, bf16[272,256]{1,0:T(8,128)(2,1)S(1)}, u32[]{:S(2)}, u32[]{:S(2)}) collective-permute-start(bf16[272,256]{1,0:T(8,128)(2,1)S(1)} %get-tuple-element.43.refs_0_), channel_id=1, source_target_pairs={{0,192},{32,224},{64,0},{96,32},{128,64},{160,96},{192,128},{224,1... | collective-permute-start | bytes 417800 | tf_op jit(solution)/shard_map/ppermute | solution.py:21
  39.0 2.2 %collective-permute-done.6.refs_1_ = bf16[272,256]{1,0:T(8,128)(2,1)S(1)} collective-permute-done((bf16[272,256]{1,0:T(8,128)(2,1)S(1)}, bf16[272,256]{1,0:T(8,128)(2,1)S(1)}, u32[]{:S(2)}, u32[]{:S(2)}) %collective-permute-start.6) | collective-permute-done | bytes 139296 | tf_op jit(solution)/shard_map/ppermute | solution.py:21
  41.2 0.3 collective-permute-start.8
  41.5 1.2 %collective-permute-start.9 = (bf16[256,256]{1,0:T(8,128)(2,1)S(1)}, bf16[256,256]{1,0:T(8,128)(2,1)S(1)}, u32[]{:S(2)}, u32[]{:S(2)}) collective-permute-start(bf16[256,256]{1,0:T(8,128)(2,1)S(1)} %get-tuple-element.44.refs_4_), channel_id=1, source_target_pairs={{0,64},{32,96},{64,128},{96,160},{128,192},{160,224},{192,0},{224,... | collective-permute-start | bytes 393224 | tf_op jit(solution)/shard_map/ppermute | solution.py:21
  42.8 1.8 %collective-permute-start.11 = (bf16[256,256]{1,0:T(8,128)(2,1)S(1)}, bf16[256,256]{1,0:T(8,128)(2,1)S(1)}, u32[]{:S(2)}, u32[]{:S(2)}) collective-permute-start(bf16[256,256]{1,0:T(8,128)(2,1)S(1)} %collective-permute-done.10.refs_6_), channel_id=1, source_target_pairs={{0,192},{32,224},{64,0},{96,32},{128,64},{160,96},{192,128},{224,1... | collective-permute-start | bytes 393224 | tf_op jit(solution)/shard_map/ppermute | solution.py:21
  44.5 5.7 %collective-permute-done.9.refs_5_ = bf16[256,256]{1,0:T(8,128)(2,1)S(1)} collective-permute-done((bf16[256,256]{1,0:T(8,128)(2,1)S(1)}, bf16[256,256]{1,0:T(8,128)(2,1)S(1)}, u32[]{:S(2)}, u32[]{:S(2)}) %collective-permute-start.9) | collective-permute-done | bytes 131104 | tf_op jit(solution)/shard_map/ppermute | solution.py:21
  50.2 0.3 choose.1
  50.5 1.2 %collective-permute-start.12 = (bf16[2,256,256]{2,1,0:T(8,128)(2,1)S(1)}, bf16[2,256,256]{2,1,0:T(8,128)(2,1)S(1)}, u32[]{:S(2)}, u32[]{:S(2)}) collective-permute-start(bf16[2,256,256]{2,1,0:T(8,128)(2,1)S(1)} %get-tuple-element.46), channel_id=1, source_target_pairs={{0,32},{32,0},{64,96},{96,64},{128,160},{160,128},{192,224},{224,1... | collective-permute-start | bytes 786440 | tf_op jit(solution)/shard_map/ppermute | solution.py:342
  51.8 1.2 %collective-permute-done.12.b_ref = bf16[2,256,256]{2,1,0:T(8,128)(2,1)S(1)} collective-permute-done((bf16[2,256,256]{2,1,0:T(8,128)(2,1)S(1)}, bf16[2,256,256]{2,1,0:T(8,128)(2,1)S(1)}, u32[]{:S(2)}, u32[]{:S(2)}) %collective-permute-start.12) | collective-permute-done | bytes 262176 | tf_op jit(solution)/shard_map/ppermute | solution.py:342
  52.9 0.7 %join.1 = bf16[2,256,256]{2,1,0:T(8,128)(2,1)} custom-call(bf16[2,256,256]{2,1,0:T(8,128)(2,1)S(1)} %get-tuple-element.45.a_ref, bf16[2,256,256]{2,1,0:T(8,128)(2,1)S(1)} %collective-permute-done.12.b_ref), custom_call_target="tpu_custom_call" | custom-call | tf_op jit(solution)/shard_map/join/pallas_call | solution.py:343
  (17 shorter events, 0.0 us)
Async XLA Ops:
  0.0 11.9 %copy-start.4 = (s32[2,256]{1,0:T(2,128)S(1)}, s32[2,256]{1,0:T(2,128)}, u32[]{:S(2)}) copy-start(s32[2,256]{1,0:T(2,128)} %slots_ref) | copy-start | bytes 6148
  0.0 9.4 %collective-permute-start = (s32[2,256]{1,0:T(2,128)}, s32[2,256]{1,0:T(2,128)S(1)}, u32[]{:S(2)}, u32[]{:S(2)}) collective-permute-start(s32[2,256]{1,0:T(2,128)} %slots_ref), channel_id=1, source_target_pairs={{0,2},{1,3},{2,4},{3,5},{4,6},{5,7},{6,8},{7,9},{8,10},{9,11},{10,... | collective-permute-start | bytes 6152 | tf_op jit(solution)/shard_map/ppermute | solution.py:32
  6.2 5.7 %collective-permute-start.1 = (s32[2,256]{1,0:T(2,128)}, s32[2,256]{1,0:T(2,128)S(1)}, u32[]{:S(2)}, u32[]{:S(2)}) collective-permute-start(s32[2,256]{1,0:T(2,128)} %slots_ref), channel_id=1, source_target_pairs={{0,32},{1,33},{2,0},{3,1},{4,2},{5,3},{6,4},{7,5},{8,6},{9,7},{10,... | collective-permute-start | bytes 6152 | tf_op jit(solution)/shard_map/ppermute | solution.py:32
  13.6 7.0 %collective-permute-start.2 = (bf16[528,256]{1,0:T(8,128)(2,1)S(1)}, bf16[528,256]{1,0:T(8,128)(2,1)S(1)}, u32[]{:S(2)}, u32[]{:S(2)}) collective-permute-start(bf16[528,256]{1,0:T(8,128)(2,1)S(1)} %get-tuple-element.29), channel_id=1, source_target_pairs={{0,1},{1,2},{2,3},{3,4},{4,5},{5,6},{6,7},{7,8},{8,9},{9,10},{10,1... | collective-permute-start | bytes 811016 | tf_op jit(solution)/shard_map/ppermute | solution.py:32
  15.3 7.8 %collective-permute-start.3 = (bf16[528,256]{1,0:T(8,128)(2,1)S(1)}, bf16[528,256]{1,0:T(8,128)(2,1)S(1)}, u32[]{:S(2)}, u32[]{:S(2)}) collective-permute-start(bf16[528,256]{1,0:T(8,128)(2,1)S(1)} %get-tuple-element.30), channel_id=1, source_target_pairs={{0,32},{1,0},{2,1},{3,2},{4,3},{5,4},{6,5},{7,6},{8,7},{9,8},{10,9... | collective-permute-start | bytes 811016 | tf_op jit(solution)/shard_map/ppermute | solution.py:32
  17.5 8.2 %copy-start.2 = (bf16[2,512,512]{2,1,0:T(8,128)(2,1)S(1)}, bf16[2,512,512]{2,1,0:T(8,128)(2,1)}, u32[]{:S(2)}) copy-start(bf16[2,512,512]{2,1,0:T(8,128)(2,1)} %by_kept_ref) | copy-start | bytes 3145732
  17.5 8.2 %copy-start.3 = (bf16[2,512,512]{2,1,0:T(8,128)(2,1)S(1)}, bf16[2,512,512]{2,1,0:T(8,128)(2,1)}, u32[]{:S(2)}) copy-start(bf16[2,512,512]{2,1,0:T(8,128)(2,1)} %by_discard_ref) | copy-start | bytes 3145732
  20.1 5.6 %copy-start = (bf16[2,512,512]{2,1,0:T(8,128)(2,1)S(1)}, bf16[2,512,512]{2,1,0:T(8,128)(2,1)}, u32[]{:S(2)}) copy-start(bf16[2,512,512]{2,1,0:T(8,128)(2,1)} %inverse_ref.2) | copy-start | bytes 3145732
  20.1 5.6 %copy-start.1 = (bf16[2,512,512]{2,1,0:T(8,128)(2,1)S(1)}, bf16[2,512,512]{2,1,0:T(8,128)(2,1)}, u32[]{:S(2)}) copy-start(bf16[2,512,512]{2,1,0:T(8,128)(2,1)} %tile_ref) | copy-start | bytes 3145732
  24.1 7.4 %collective-permute-start.4 = (bf16[2,256,256]{2,1,0:T(8,128)(2,1)S(1)}, bf16[2,256,256]{2,1,0:T(8,128)(2,1)S(1)}, u32[]{:S(2)}, u32[]{:S(2)}) collective-permute-start(bf16[2,256,256]{2,1,0:T(8,128)(2,1)S(1)} %get-tuple-element.41), channel_id=1, source_target_pairs={{0,1},{1,2},{2,3},{3,4},{4,5},{5,6},{6,7},{7,8},{8,9},{9,10},{10,1... | collective-permute-start | bytes 786440 | tf_op jit(solution)/shard_map/ppermute | solution.py:32
  25.7 8.6 %copy-start.5 = (s32[2]{0:T(128)S(1)}, s32[2]{0:T(128)}, u32[]{:S(2)}) copy-start(s32[2]{0:T(128)} %length_ref.1) | copy-start | bytes 28
  25.7 8.6 %copy-start.6 = (s32[2]{0:T(128)S(1)}, s32[2]{0:T(128)}, u32[]{:S(2)}) copy-start(s32[2]{0:T(128)} %code_ref.1) | copy-start | bytes 28
  25.7 8.6 %collective-permute-start.5 = (bf16[2,256,256]{2,1,0:T(8,128)(2,1)S(1)}, bf16[2,256,256]{2,1,0:T(8,128)(2,1)S(1)}, u32[]{:S(2)}, u32[]{:S(2)}) collective-permute-start(bf16[2,256,256]{2,1,0:T(8,128)(2,1)S(1)} %get-tuple-element.42), channel_id=1, source_target_pairs={{0,32},{1,0},{2,1},{3,2},{4,3},{5,4},{6,5},{7,6},{8,7},{9,8},{10,9... | collective-permute-start | bytes 786440 | tf_op jit(solution)/shard_map/ppermute | solution.py:32
  35.0 6.2 %collective-permute-start.6 = (bf16[272,256]{1,0:T(8,128)(2,1)S(1)}, bf16[272,256]{1,0:T(8,128)(2,1)S(1)}, u32[]{:S(2)}, u32[]{:S(2)}) collective-permute-start(bf16[272,256]{1,0:T(8,128)(2,1)S(1)} %get-tuple-element.43.refs_0_), channel_id=1, source_target_pairs={{0,64},{32,96},{64,128},{96,160},{128,192},{160,224},{192,0},{224,... | collective-permute-start | bytes 417800 | tf_op jit(solution)/shard_map/ppermute | solution.py:21
  36.3 6.5 %collective-permute-start.10 = (bf16[256,256]{1,0:T(8,128)(2,1)S(1)}, bf16[256,256]{1,0:T(8,128)(2,1)S(1)}, u32[]{:S(2)}, u32[]{:S(2)}) collective-permute-start(bf16[256,256]{1,0:T(8,128)(2,1)S(1)} %get-tuple-element.44.refs_4_), channel_id=1, source_target_pairs={{0,192},{32,224},{64,0},{96,32},{128,64},{160,96},{192,128},{224,1... | collective-permute-start | bytes 393224 | tf_op jit(solution)/shard_map/ppermute | solution.py:21
  37.8 12.4 %collective-permute-start.7 = (bf16[272,256]{1,0:T(8,128)(2,1)S(1)}, bf16[272,256]{1,0:T(8,128)(2,1)S(1)}, u32[]{:S(2)}, u32[]{:S(2)}) collective-permute-start(bf16[272,256]{1,0:T(8,128)(2,1)S(1)} %get-tuple-element.43.refs_0_), channel_id=1, source_target_pairs={{0,192},{32,224},{64,0},{96,32},{128,64},{160,96},{192,128},{224,1... | collective-permute-start | bytes 417800 | tf_op jit(solution)/shard_map/ppermute | solution.py:21
  41.2 9.0 %collective-permute-start.8 = (bf16[272,256]{1,0:T(8,128)(2,1)S(1)}, bf16[272,256]{1,0:T(8,128)(2,1)S(1)}, u32[]{:S(2)}, u32[]{:S(2)}) collective-permute-start(bf16[272,256]{1,0:T(8,128)(2,1)S(1)} %collective-permute-done.6.refs_1_), channel_id=1, source_target_pairs={{0,64},{32,96},{64,128},{96,160},{128,192},{160,224},{192,0},{224,... | collective-permute-start | bytes 417800 | tf_op jit(solution)/shard_map/ppermute | solution.py:21
  41.5 8.7 %collective-permute-start.9 = (bf16[256,256]{1,0:T(8,128)(2,1)S(1)}, bf16[256,256]{1,0:T(8,128)(2,1)S(1)}, u32[]{:S(2)}, u32[]{:S(2)}) collective-permute-start(bf16[256,256]{1,0:T(8,128)(2,1)S(1)} %get-tuple-element.44.refs_4_), channel_id=1, source_target_pairs={{0,64},{32,96},{64,128},{96,160},{128,192},{160,224},{192,0},{224,... | collective-permute-start | bytes 393224 | tf_op jit(solution)/shard_map/ppermute | solution.py:21
  42.8 7.4 %collective-permute-start.11 = (bf16[256,256]{1,0:T(8,128)(2,1)S(1)}, bf16[256,256]{1,0:T(8,128)(2,1)S(1)}, u32[]{:S(2)}, u32[]{:S(2)}) collective-permute-start(bf16[256,256]{1,0:T(8,128)(2,1)S(1)} %collective-permute-done.10.refs_6_), channel_id=1, source_target_pairs={{0,192},{32,224},{64,0},{96,32},{128,64},{160,96},{192,128},{224,1... | collective-permute-start | bytes 393224 | tf_op jit(solution)/shard_map/ppermute | solution.py:21
  50.5 2.4 %collective-permute-start.12 = (bf16[2,256,256]{2,1,0:T(8,128)(2,1)S(1)}, bf16[2,256,256]{2,1,0:T(8,128)(2,1)S(1)}, u32[]{:S(2)}, u32[]{:S(2)}) collective-permute-start(bf16[2,256,256]{2,1,0:T(8,128)(2,1)S(1)} %get-tuple-element.46), channel_id=1, source_target_pairs={{0,32},{32,0},{64,96},{96,64},{128,160},{160,128},{192,224},{224,1... | collective-permute-start | bytes 786440 | tf_op jit(solution)/shard_map/ppermute | solution.py:342

commit v4 on v3

--- a/solution.py
+++ b/solution.py
@@ -21,12 +21,12 @@
     return lax.ppermute(value, axis, [(i, (i + by) % length) for i in range(length)])
 
 
-def turn(value, by):
+def swap(value, by, parity):
     regions, length = lax.axis_size("region"), lax.axis_size("box")
     pairs = []
     for r in range(regions):
         for j in range(length):
-            there = j + (by if r % 2 == 0 else -by)
+            there = j + by if j // by % 2 == parity else j - by
             goal = (r, there) if 0 <= there < length else (r + 1 - 2 * (r % 2), j)
             pairs.append((r * length + j, goal[0] * length + goal[1]))
     return lax.ppermute(value, ("region", "box"), pairs)
@@ -48,7 +48,9 @@
     return columns, rows
 
 
-def self_kernel(slots_ref, tile_ref, inverse_ref, by_kept_ref, by_discard_ref, base_ref):
+def self_kernel(
+    length_ref, code_ref, slots_ref, tile_ref, inverse_ref, by_kept_ref, by_discard_ref, base_ref, keep_ref, codes_ref
+):
     place = pl.program_id(0)
     slots = jnp.where(place == 0, slots_ref[0:1, :], slots_ref[1:2, :])
     columns, rows = pickers(slots, tile_ref.shape[1])
@@ -57,11 +59,20 @@
     left = dot(rows, by_discard_ref[0]).astype(jnp.bfloat16)
     tile = dot(rows, dot(tile_ref[0], columns).astype(jnp.bfloat16))
     base_ref[0] = tile - dot(left, solved)
+    row = lax.broadcasted_iota(jnp.int32, keep_ref.shape[1:], 0)
+    column = lax.broadcasted_iota(jnp.int32, keep_ref.shape[1:], 1)
+    length = length_ref[place]
+    keep_ref[0] = jnp.where((row < length) & (column < length), 1.0, 0.0)
+
+    @pl.when(place == 0)
+    def _():
+        row = lax.broadcasted_iota(jnp.int32, codes_ref.shape, 0)
+        codes_ref[...] = jnp.where(row == 0, code_ref[0], code_ref[1]).astype(jnp.float32).astype(jnp.bfloat16)
 
 
 def directions():
-    core = lax.rem(lax.axis_index("region"), 2)
-    return core, 1 - core
+    odd = lax.rem(lax.axis_index("box"), 2)
+    return 1 - odd, odd
 
 
 def load_kernel(first, *refs):
@@ -143,7 +154,9 @@
 
 def far_kernel(one_ref, two_ref, own_ref, site_ref, reduced, left, out_one, out_two):
     span = own_ref.shape[1]
-    from_there = (two_ref[...], one_ref[...])
+    position = lax.axis_index("box")
+    inner = lax.rem(lax.div(position + 1, 2), 2) == 1
+    from_there = [jnp.where(inner, a[...], b[...]) for a, b in ((one_ref, two_ref), (two_ref, one_ref))]
     targets = targets_of(2, site_ref)
     picks = []
     for which in range(2):
@@ -173,29 +186,23 @@
     passed = (one_ref, two_ref)
     picks = []
     for which in range(2):
-        code = passed[1 - which][2 * span :].astype(jnp.float32).astype(jnp.int32)
+        code = passed[which][2 * span :].astype(jnp.float32).astype(jnp.int32)
         slots = code[0:2] * 2 + code[2:4]
         picks += [pickers(slots[t : t + 1], near_ref.shape[1]) for t in range(2)]
     half = [dot(near_ref[at], picks[at][0]).astype(jnp.bfloat16) for at in range(4)]
     near = [dot(picks[at][1], half[at]) for at in range(4)]
     for which, out in enumerate((out_one, out_two)):
         for t in range(2):
-            far = passed[which][t * span : (t + 1) * span].astype(jnp.float32)
+            far = passed[1 - which][t * span : (t + 1) * span].astype(jnp.float32)
             out[t] = (near[2 * which + t] + far).astype(jnp.bfloat16)
 
 
-def child_kernel(length_ref, code_ref, base_ref, one_ref, two_ref, *outs):
+def child_kernel(base_ref, keep_ref, codes_ref, one_ref, two_ref, *outs):
     places, span = base_ref.shape[:2]
-    row = lax.broadcasted_iota(jnp.int32, (span, span), 0)
-    column = lax.broadcasted_iota(jnp.int32, (span, span), 1)
     for place in range(places):
         value = base_ref[place] - one_ref[place].astype(jnp.float32) - two_ref[place].astype(jnp.float32)
-        length = length_ref[place]
-        valid = (row < length) & (column < length)
-        outs[place][0:span] = jnp.where(valid, value, 0.0).astype(jnp.bfloat16)
-    row = lax.broadcasted_iota(jnp.int32, (CODE_ROWS, span), 0)
-    code = jnp.where(row == 0, code_ref[0], code_ref[1])
-    outs[0][span:] = code.astype(jnp.float32).astype(jnp.bfloat16)
+        outs[place][0:span] = (value * keep_ref[place]).astype(jnp.bfloat16)
+    outs[0][span:] = codes_ref[...]
 
 
 def choose_kernel(*refs):
@@ -241,15 +248,16 @@
     def block(rows, columns):
         return pl.BlockSpec((1, rows, columns), lambda l: (l, 0, 0))
 
-    own = (retained_slots, kept_diagonal_tile, discard_reciprocal, discard_by_kept, kept_by_discard)
+    own = (kept_list_length, ancestor_site_map, retained_slots, kept_diagonal_tile, discard_reciprocal, discard_by_kept, kept_by_discard)
 
     def self_update(*own):
         return pl.pallas_call(
             self_kernel,
             grid=(places,),
-            in_specs=[VMEM, block(wide, wide), block(tall, tall), block(tall, wide), block(wide, tall)],
-            out_specs=block(tile_span, tile_span),
-            out_shape=jax.ShapeDtypeStruct((places, tile_span, tile_span), jnp.float32),
+            in_specs=[SMEM, SMEM, VMEM, block(wide, wide), block(tall, tall), block(tall, wide), block(wide, tall)],
+            out_specs=[block(tile_span, tile_span)] * 2 + [pl.BlockSpec((CODE_ROWS, tile_span), lambda l: (0, 0))],
+            out_shape=[jax.ShapeDtypeStruct((places, tile_span, tile_span), jnp.float32)] * 2
+            + [jax.ShapeDtypeStruct((CODE_ROWS, tile_span), jnp.bfloat16)],
             compiler_params=params,
             name="self_update",
         )(*own)
@@ -267,7 +275,8 @@
         )(*[pltpu.with_memory_space_constraint(v, pltpu.HBM) for v in sources])
 
     coupled = (adjacent_kept_to_discard, adjacent_discard_to_kept)
-    far_slots = [turn(retained_slots, by) for by in (2, -2)]
+    outer_slots = swap(retained_slots, 2, 1)
+    far_slots = [swap(retained_slots, 2, 0), outer_slots]
     far_sources = (adjacent_site_table, discard_reciprocal) + coupled
     rights, lefts = (4, tall, wide), (4, wide, tall)
     site, inverse, reduced, far_left = pl.pallas_call(
@@ -293,7 +302,7 @@
         compiler_params=params,
         name="far_update",
     )(*far_slots, retained_slots, site, reduced, far_left)
-    passed = [turn(value, by) for value, by in zip(far, (1, -1))]
+    passed = [swap(value, 1, parity) for value, parity in zip(far, (1, 0))]
     coupled, own, far = lax.optimization_barrier((coupled, own, far))
     near_pair = load(0, coupled)
     whole = pl.pallas_call(
@@ -312,19 +321,19 @@
         compiler_params=params,
         name="near_update",
     )(*passed, whole)
-    arrived = [turn(sent[0], 1), turn(sent[1], -1)]
+    arrived = [swap(sent[0], 1, 1), swap(sent[1], 1, 0)]
     base = self_update(*own)
 
     half = jax.ShapeDtypeStruct((tile_span, tile_span), jnp.bfloat16)
     coded = jax.ShapeDtypeStruct((tile_span + CODE_ROWS, tile_span), jnp.bfloat16)
     one, two = pl.pallas_call(
         child_kernel,
-        in_specs=[SMEM, SMEM] + [VMEM] * 3,
+        in_specs=[VMEM] * 5,
         out_specs=[VMEM] * 2,
         out_shape=[coded, half],
         compiler_params=params,
         name="child",
-    )(kept_list_length, ancestor_site_map, base, *arrived)
+    )(*base, *arrived)
 
     one_back, two_ahead = shift(one, "region", 2), shift(two, "region", -2)
     two_back, one_ahead = shift(two, "region", 2), shift(one, "region", -2)

time: 53.7 us -> 50.3 us (0.937)
  waiting for transfers between devices: 20.6 us -> 11.7 us
  starting transfers between devices: 18 us -> 23.2 us
    ppermute x6, waiting for transfers between devices: 11.5 us -> 5.57 us  [swap(): return lax.ppermute(value, ('region', 'box'), pairs)]
    ppermute x1, starting transfers between devices: 1.22 us -> 5.74 us  [local(): received = lax.ppermute(other, 'region', partners)]
    ppermute x6, waiting for transfers between devices: 7.88 us -> 4.99 us  [shift(): lax.ppermute(value, axis, [(i, (i + by) % length) for i in range(length)])]
    ppermute x6, starting transfers between devices: 9.47 us -> 10.7 us  [swap(): return lax.ppermute(value, ('region', 'box'), pairs)]
    ppermute x6, starting transfers between devices: 7.33 us -> 6.73 us  [shift(): lax.ppermute(value, axis, [(i, (i + by) % length) for i in range(length)])]
  transfers between devices with their start and end apart: 13 -> 13, of which waited for: 8 -> 5; matrix products, arithmetic and copies ran while one was open for 0% -> 0% of each run, Pallas kernels for 19% -> 22%
where the time goes in v4:
time: 50.3 us; the launch traced here: 50 us
  starting transfers between devices  23.2 us (46%)
  Pallas kernels  14.9 us (30%)
  waiting for transfers between devices  11.7 us (23%)
    ppermute x6, starting transfers between devices, swap(): return lax.ppermute(value, ('region', 'box'), pairs)  10.7 us
    ppermute x6, starting transfers between devices, shift(): lax.ppermute(value, axis, [(i, (i + by) % length) for i in range(length)])  6.73 us
    ppermute x1, starting transfers between devices, local(): received = lax.ppermute(other, 'region', partners)  5.74 us
    ppermute x6, waiting for transfers between devices, swap(): return lax.ppermute(value, ('region', 'box'), pairs)  5.57 us
    ppermute x6, waiting for transfers between devices, shift(): lax.ppermute(value, axis, [(i, (i + by) % length) for i in range(length)])  4.99 us
    pallas_call x1, Pallas kernels, local(): pl.pallas_call(functools.partial(reduce_kernel, 2), in_specs=[HBM] * 4, o...  3.22 us
    pallas_call x1, Pallas kernels, self_update(): pl.pallas_call(self_kernel, grid=(places,), in_specs=[SMEM, SMEM, VMEM, b...  2.94 us
    pallas_call x1, Pallas kernels, local(): pl.pallas_call(whole_kernel, in_specs=[VMEM] * 4, out_specs=VMEM, out_sha...  2.59 us
  transfers between devices with their start and end apart: 13, of which 5 were waited for; matrix products, arithmetic and copies ran while one was open for 0% of the time, Pallas kernels for 22%

profile of v4, /device:TPU:25, one launch (start us, length us, event | category | flops | bytes accessed | tf_op | source)
XLA Modules:
  0.0 50.0 jit_solution(7223450185915933660)
XLA Ops:
  0.0 3.0 %collective-permute-start = (s32[2,256]{1,0:T(2,128)}, s32[2,256]{1,0:T(2,128)S(1)}, u32[]{:S(2)}, u32[]{:S(2)}) collective-permute-start(s32[2,256]{1,0:T(2,128)} %slots_ref), channel_id=1, source_target_pairs={{0,2},{1,3},{2,0},{3,1},{4,6},{5,7},{6,4},{7,5},{8,10},{9,11},{10,... | collective-permute-start | bytes 6152 | tf_op jit(solution)/shard_map/ppermute | solution.py:32
  3.0 4.4 %collective-permute-start.1 = (s32[2,256]{1,0:T(2,128)}, s32[2,256]{1,0:T(2,128)S(1)}, u32[]{:S(2)}, u32[]{:S(2)}) collective-permute-start(s32[2,256]{1,0:T(2,128)} %slots_ref), channel_id=1, source_target_pairs={{0,32},{1,33},{2,4},{3,5},{4,2},{5,3},{6,8},{7,9},{8,6},{9,7},{10,... | collective-permute-start | bytes 6152 | tf_op jit(solution)/shard_map/ppermute | solution.py:32
  7.4 3.2 %load_reduce.1 = (s32[2,4]{1,0:T(2,128)S(1)}, bf16[2,512,512]{2,1,0:T(8,128)(2,1)S(1)}, bf16[4,512,512]{2,1,0:T(8,128)(2,1)S(1)}, bf16[4,512,512]{2,1,0:T(8,128)(2,1)S(1)}) custom-call(s32[2,4]{1,0:T(2,128)} %table_ref.1, bf16[2,512,512]{2,1,0:T(8,128)(2,1)} %inverse_ref.2, bf16[2,4,512,512]{3,2,1,0:T(8,128)(2,1)} %refs_0_, bf16[2,4,512,512]{3,2,1,0:T(8,128)(2,1)} %refs_1_), custom_call_target="tpu_custom_call" | custom-call | tf_op jit(solution)/shard_map/load_reduce/pallas_call | solution.py:282
  10.6 1.7 %far_update.1 = (bf16[528,256]{1,0:T(8,128)(2,1)S(1)}, bf16[528,256]{1,0:T(8,128)(2,1)S(1)}) custom-call(s32[2,256]{1,0:T(2,128)S(1)} %collective-permute-done.one_ref, s32[2,256]{1,0:T(2,128)S(1)} %collective-permute-done.1.two_ref, s32[2,256]{1,0:T(2,128)S(1)} %copy-done.4, s32[2,4]{1,0:T(2,128)S(1)} %get-tuple-element.31.site_ref, ...), custom_call_target="tpu_custom_call" | custom-call | tf_op jit(solution)/shard_map/far_update/pallas_call | solution.py:297
  12.3 2.0 %collective-permute-start.2 = (bf16[528,256]{1,0:T(8,128)(2,1)S(1)}, bf16[528,256]{1,0:T(8,128)(2,1)S(1)}, u32[]{:S(2)}, u32[]{:S(2)}) collective-permute-start(bf16[528,256]{1,0:T(8,128)(2,1)S(1)} %get-tuple-element.34), channel_id=1, source_target_pairs={{0,32},{1,2},{2,1},{3,4},{4,3},{5,6},{6,5},{7,8},{8,7},{9,10},{10,... | collective-permute-start | bytes 811016 | tf_op jit(solution)/shard_map/ppermute | solution.py:32
  14.4 2.2 %load.1 = (bf16[4,512,512]{2,1,0:T(8,128)(2,1)S(1)}, bf16[4,512,512]{2,1,0:T(8,128)(2,1)S(1)}) custom-call(bf16[2,4,512,512]{3,2,1,0:T(8,128)(2,1)} %refs_0_, bf16[2,4,512,512]{3,2,1,0:T(8,128)(2,1)} %refs_1_), custom_call_target="tpu_custom_call" | custom-call | tf_op jit(solution)/shard_map/load/pallas_call | solution.py:267
  16.6 0.0 copy-start.2
  16.6 0.0 copy-start.3
  16.6 2.6 %whole_update.1.near_ref = bf16[4,512,512]{2,1,0:T(8,128)(2,1)S(1)} custom-call(s32[2,4]{1,0:T(2,128)S(1)} %get-tuple-element.31.site_ref, bf16[2,512,512]{2,1,0:T(8,128)(2,1)S(1)} %get-tuple-element.46.inverse, bf16[4,512,512]{2,1,0:T(8,128)(2,1)S(1)} %get-tuple-element.49.right, bf16[4,512,512]{2,1,0:T(8,128)(2,1)S(1)} %get-tuple-element.50.left), custom_call_target="tpu_custom_call" | custom-call | tf_op jit(solution)/shard_map/whole_update/pallas_call | solution.py:308
  19.2 0.0 copy-start
  19.2 0.0 copy-start.1
  19.3 0.0 copy-start.5
  19.3 0.0 copy-start.6
  19.3 2.0 %collective-permute-done.2.one_ref = bf16[528,256]{1,0:T(8,128)(2,1)S(1)} collective-permute-done((bf16[528,256]{1,0:T(8,128)(2,1)S(1)}, bf16[528,256]{1,0:T(8,128)(2,1)S(1)}, u32[]{:S(2)}, u32[]{:S(2)}) %collective-permute-start.2) | collective-permute-done | bytes 270368 | tf_op jit(solution)/shard_map/ppermute | solution.py:32
  21.3 1.1 %near_update.1 = (bf16[2,256,256]{2,1,0:T(8,128)(2,1)S(1)}, bf16[2,256,256]{2,1,0:T(8,128)(2,1)S(1)}) custom-call(bf16[528,256]{1,0:T(8,128)(2,1)S(1)} %collective-permute-done.2.one_ref, bf16[528,256]{1,0:T(8,128)(2,1)S(1)} %collective-permute-done.3.two_ref, bf16[4,512,512]{2,1,0:T(8,128)(2,1)S(1)} %whole_update.1.near_ref), custom_call_target="tpu_custom_call" | custom-call | tf_op jit(solution)/shard_map/near_update/pallas_call | solution.py:316
  22.4 1.3 %collective-permute-start.4 = (bf16[2,256,256]{2,1,0:T(8,128)(2,1)S(1)}, bf16[2,256,256]{2,1,0:T(8,128)(2,1)S(1)}, u32[]{:S(2)}, u32[]{:S(2)}) collective-permute-start(bf16[2,256,256]{2,1,0:T(8,128)(2,1)S(1)} %get-tuple-element.51), channel_id=1, source_target_pairs={{0,32},{1,2},{2,1},{3,4},{4,3},{5,6},{6,5},{7,8},{8,7},{9,10},{10,... | collective-permute-start | bytes 786440 | tf_op jit(solution)/shard_map/ppermute | solution.py:32
  23.6 0.0 collective-permute-start.5
  23.7 2.9 %self_update.1 = (f32[2,256,256]{2,1,0:T(8,128)S(1)}, f32[2,256,256]{2,1,0:T(8,128)S(1)}, bf16[16,256]{1,0:T(8,128)(2,1)S(1)}) custom-call(s32[2]{0:T(128)S(1)} %copy-done.5, s32[2]{0:T(128)S(1)} %copy-done.6, s32[2,256]{1,0:T(2,128)S(1)} %copy-done.4, bf16[2,512,512]{2,1,0:T(8,128)(2,1)S(1)} %copy-done.1, bf16[2,512,512]{2,1,0:T(8,128)(2,1)S(1)} %copy-done, ...), custom_call_target="tpu_custom_call" | custom-call | tf_op jit(solution)/shard_map/self_update/pallas_call | solution.py:254
  26.6 3.6 %collective-permute-done.4.one_ref = bf16[2,256,256]{2,1,0:T(8,128)(2,1)S(1)} collective-permute-done((bf16[2,256,256]{2,1,0:T(8,128)(2,1)S(1)}, bf16[2,256,256]{2,1,0:T(8,128)(2,1)S(1)}, u32[]{:S(2)}, u32[]{:S(2)}) %collective-permute-start.4) | collective-permute-done | bytes 262176 | tf_op jit(solution)/shard_map/ppermute | solution.py:32
  30.2 0.1 child.1
  30.3 1.3 %collective-permute-start.6 = (bf16[272,256]{1,0:T(8,128)(2,1)S(1)}, bf16[272,256]{1,0:T(8,128)(2,1)S(1)}, u32[]{:S(2)}, u32[]{:S(2)}) collective-permute-start(bf16[272,256]{1,0:T(8,128)(2,1)S(1)} %get-tuple-element.53.refs_0_), channel_id=1, source_target_pairs={{0,64},{32,96},{64,128},{96,160},{128,192},{160,224},{192,0},{224,... | collective-permute-start | bytes 417800 | tf_op jit(solution)/shard_map/ppermute | solution.py:21
  31.6 1.5 %collective-permute-start.10 = (bf16[256,256]{1,0:T(8,128)(2,1)S(1)}, bf16[256,256]{1,0:T(8,128)(2,1)S(1)}, u32[]{:S(2)}, u32[]{:S(2)}) collective-permute-start(bf16[256,256]{1,0:T(8,128)(2,1)S(1)} %get-tuple-element.54.refs_4_), channel_id=1, source_target_pairs={{0,192},{32,224},{64,0},{96,32},{128,64},{160,96},{192,128},{224,1... | collective-permute-start | bytes 393224 | tf_op jit(solution)/shard_map/ppermute | solution.py:21
  33.0 1.3 %collective-permute-start.7 = (bf16[272,256]{1,0:T(8,128)(2,1)S(1)}, bf16[272,256]{1,0:T(8,128)(2,1)S(1)}, u32[]{:S(2)}, u32[]{:S(2)}) collective-permute-start(bf16[272,256]{1,0:T(8,128)(2,1)S(1)} %get-tuple-element.53.refs_0_), channel_id=1, source_target_pairs={{0,192},{32,224},{64,0},{96,32},{128,64},{160,96},{192,128},{224,1... | collective-permute-start | bytes 417800 | tf_op jit(solution)/shard_map/ppermute | solution.py:21
  34.3 1.2 %collective-permute-done.6.refs_1_ = bf16[272,256]{1,0:T(8,128)(2,1)S(1)} collective-permute-done((bf16[272,256]{1,0:T(8,128)(2,1)S(1)}, bf16[272,256]{1,0:T(8,128)(2,1)S(1)}, u32[]{:S(2)}, u32[]{:S(2)}) %collective-permute-start.6) | collective-permute-done | bytes 139296 | tf_op jit(solution)/shard_map/ppermute | solution.py:21
  35.5 0.0 collective-permute-start.8
  35.5 1.2 %collective-permute-start.9 = (bf16[256,256]{1,0:T(8,128)(2,1)S(1)}, bf16[256,256]{1,0:T(8,128)(2,1)S(1)}, u32[]{:S(2)}, u32[]{:S(2)}) collective-permute-start(bf16[256,256]{1,0:T(8,128)(2,1)S(1)} %get-tuple-element.54.refs_4_), channel_id=1, source_target_pairs={{0,64},{32,96},{64,128},{96,160},{128,192},{160,224},{192,0},{224,... | collective-permute-start | bytes 393224 | tf_op jit(solution)/shard_map/ppermute | solution.py:21
  36.7 1.5 %collective-permute-start.11 = (bf16[256,256]{1,0:T(8,128)(2,1)S(1)}, bf16[256,256]{1,0:T(8,128)(2,1)S(1)}, u32[]{:S(2)}, u32[]{:S(2)}) collective-permute-start(bf16[256,256]{1,0:T(8,128)(2,1)S(1)} %collective-permute-done.10.refs_6_), channel_id=1, source_target_pairs={{0,192},{32,224},{64,0},{96,32},{128,64},{160,96},{192,128},{224,1... | collective-permute-start | bytes 393224 | tf_op jit(solution)/shard_map/ppermute | solution.py:21
  38.2 3.8 %collective-permute-done.9.refs_5_ = bf16[256,256]{1,0:T(8,128)(2,1)S(1)} collective-permute-done((bf16[256,256]{1,0:T(8,128)(2,1)S(1)}, bf16[256,256]{1,0:T(8,128)(2,1)S(1)}, u32[]{:S(2)}, u32[]{:S(2)}) %collective-permute-start.9) | collective-permute-done | bytes 131104 | tf_op jit(solution)/shard_map/ppermute | solution.py:21
  42.0 0.4 choose.1
  42.4 5.7 %collective-permute-start.12 = (bf16[2,256,256]{2,1,0:T(8,128)(2,1)S(1)}, bf16[2,256,256]{2,1,0:T(8,128)(2,1)S(1)}, u32[]{:S(2)}, u32[]{:S(2)}) collective-permute-start(bf16[2,256,256]{2,1,0:T(8,128)(2,1)S(1)} %get-tuple-element.56), channel_id=1, source_target_pairs={{0,32},{32,0},{64,96},{96,64},{128,160},{160,128},{192,224},{224,1... | collective-permute-start | bytes 786440 | tf_op jit(solution)/shard_map/ppermute | solution.py:351
  48.1 1.2 %collective-permute-done.12.b_ref = bf16[2,256,256]{2,1,0:T(8,128)(2,1)S(1)} collective-permute-done((bf16[2,256,256]{2,1,0:T(8,128)(2,1)S(1)}, bf16[2,256,256]{2,1,0:T(8,128)(2,1)S(1)}, u32[]{:S(2)}, u32[]{:S(2)}) %collective-permute-start.12) | collective-permute-done | bytes 262176 | tf_op jit(solution)/shard_map/ppermute | solution.py:351
  49.3 0.7 %join.1 = bf16[2,256,256]{2,1,0:T(8,128)(2,1)} custom-call(bf16[2,256,256]{2,1,0:T(8,128)(2,1)S(1)} %get-tuple-element.55.a_ref, bf16[2,256,256]{2,1,0:T(8,128)(2,1)S(1)} %collective-permute-done.12.b_ref), custom_call_target="tpu_custom_call" | custom-call | tf_op jit(solution)/shard_map/join/pallas_call | solution.py:352
  (17 shorter events, 0.0 us)
Async XLA Ops:
  0.0 10.6 %copy-start.4 = (s32[2,256]{1,0:T(2,128)S(1)}, s32[2,256]{1,0:T(2,128)}, u32[]{:S(2)}) copy-start(s32[2,256]{1,0:T(2,128)} %slots_ref) | copy-start | bytes 6148
  0.0 10.6 %collective-permute-start = (s32[2,256]{1,0:T(2,128)}, s32[2,256]{1,0:T(2,128)S(1)}, u32[]{:S(2)}, u32[]{:S(2)}) collective-permute-start(s32[2,256]{1,0:T(2,128)} %slots_ref), channel_id=1, source_target_pairs={{0,2},{1,3},{2,0},{3,1},{4,6},{5,7},{6,4},{7,5},{8,10},{9,11},{10,... | collective-permute-start | bytes 6152 | tf_op jit(solution)/shard_map/ppermute | solution.py:32
  3.0 7.6 %collective-permute-start.1 = (s32[2,256]{1,0:T(2,128)}, s32[2,256]{1,0:T(2,128)S(1)}, u32[]{:S(2)}, u32[]{:S(2)}) collective-permute-start(s32[2,256]{1,0:T(2,128)} %slots_ref), channel_id=1, source_target_pairs={{0,32},{1,33},{2,4},{3,5},{4,2},{5,3},{6,8},{7,9},{8,6},{9,7},{10,... | collective-permute-start | bytes 6152 | tf_op jit(solution)/shard_map/ppermute | solution.py:32
  12.3 8.9 %collective-permute-start.2 = (bf16[528,256]{1,0:T(8,128)(2,1)S(1)}, bf16[528,256]{1,0:T(8,128)(2,1)S(1)}, u32[]{:S(2)}, u32[]{:S(2)}) collective-permute-start(bf16[528,256]{1,0:T(8,128)(2,1)S(1)} %get-tuple-element.34), channel_id=1, source_target_pairs={{0,32},{1,2},{2,1},{3,4},{4,3},{5,6},{6,5},{7,8},{8,7},{9,10},{10,... | collective-permute-start | bytes 811016 | tf_op jit(solution)/shard_map/ppermute | solution.py:32
  14.4 6.9 %collective-permute-start.3 = (bf16[528,256]{1,0:T(8,128)(2,1)S(1)}, bf16[528,256]{1,0:T(8,128)(2,1)S(1)}, u32[]{:S(2)}, u32[]{:S(2)}) collective-permute-start(bf16[528,256]{1,0:T(8,128)(2,1)S(1)} %get-tuple-element.35), channel_id=1, source_target_pairs={{0,1},{1,0},{2,3},{3,2},{4,5},{5,4},{6,7},{7,6},{8,9},{9,8},{10,11... | collective-permute-start | bytes 811016 | tf_op jit(solution)/shard_map/ppermute | solution.py:32
  16.6 7.0 %copy-start.2 = (bf16[2,512,512]{2,1,0:T(8,128)(2,1)S(1)}, bf16[2,512,512]{2,1,0:T(8,128)(2,1)}, u32[]{:S(2)}) copy-start(bf16[2,512,512]{2,1,0:T(8,128)(2,1)} %by_kept_ref) | copy-start | bytes 3145732
  16.6 7.0 %copy-start.3 = (bf16[2,512,512]{2,1,0:T(8,128)(2,1)S(1)}, bf16[2,512,512]{2,1,0:T(8,128)(2,1)}, u32[]{:S(2)}) copy-start(bf16[2,512,512]{2,1,0:T(8,128)(2,1)} %by_discard_ref) | copy-start | bytes 3145732
  19.2 4.4 %copy-start = (bf16[2,512,512]{2,1,0:T(8,128)(2,1)S(1)}, bf16[2,512,512]{2,1,0:T(8,128)(2,1)}, u32[]{:S(2)}) copy-start(bf16[2,512,512]{2,1,0:T(8,128)(2,1)} %inverse_ref.2) | copy-start | bytes 3145732
  19.2 4.4 %copy-start.1 = (bf16[2,512,512]{2,1,0:T(8,128)(2,1)S(1)}, bf16[2,512,512]{2,1,0:T(8,128)(2,1)}, u32[]{:S(2)}) copy-start(bf16[2,512,512]{2,1,0:T(8,128)(2,1)} %tile_ref) | copy-start | bytes 3145732
  19.3 4.4 %copy-start.5 = (s32[2]{0:T(128)S(1)}, s32[2]{0:T(128)}, u32[]{:S(2)}) copy-start(s32[2]{0:T(128)} %length_ref) | copy-start | bytes 28
  19.3 4.4 %copy-start.6 = (s32[2]{0:T(128)S(1)}, s32[2]{0:T(128)}, u32[]{:S(2)}) copy-start(s32[2]{0:T(128)} %code_ref) | copy-start | bytes 28
  22.4 7.8 %collective-permute-start.4 = (bf16[2,256,256]{2,1,0:T(8,128)(2,1)S(1)}, bf16[2,256,256]{2,1,0:T(8,128)(2,1)S(1)}, u32[]{:S(2)}, u32[]{:S(2)}) collective-permute-start(bf16[2,256,256]{2,1,0:T(8,128)(2,1)S(1)} %get-tuple-element.51), channel_id=1, source_target_pairs={{0,32},{1,2},{2,1},{3,4},{4,3},{5,6},{6,5},{7,8},{8,7},{9,10},{10,... | collective-permute-start | bytes 786440 | tf_op jit(solution)/shard_map/ppermute | solution.py:32
  23.6 6.6 %collective-permute-start.5 = (bf16[2,256,256]{2,1,0:T(8,128)(2,1)S(1)}, bf16[2,256,256]{2,1,0:T(8,128)(2,1)S(1)}, u32[]{:S(2)}, u32[]{:S(2)}) collective-permute-start(bf16[2,256,256]{2,1,0:T(8,128)(2,1)S(1)} %get-tuple-element.52), channel_id=1, source_target_pairs={{0,1},{1,0},{2,3},{3,2},{4,5},{5,4},{6,7},{7,6},{8,9},{9,8},{10,11... | collective-permute-start | bytes 786440 | tf_op jit(solution)/shard_map/ppermute | solution.py:32
  30.3 5.2 %collective-permute-start.6 = (bf16[272,256]{1,0:T(8,128)(2,1)S(1)}, bf16[272,256]{1,0:T(8,128)(2,1)S(1)}, u32[]{:S(2)}, u32[]{:S(2)}) collective-permute-start(bf16[272,256]{1,0:T(8,128)(2,1)S(1)} %get-tuple-element.53.refs_0_), channel_id=1, source_target_pairs={{0,64},{32,96},{64,128},{96,160},{128,192},{160,224},{192,0},{224,... | collective-permute-start | bytes 417800 | tf_op jit(solution)/shard_map/ppermute | solution.py:21
  31.6 5.1 %collective-permute-start.10 = (bf16[256,256]{1,0:T(8,128)(2,1)S(1)}, bf16[256,256]{1,0:T(8,128)(2,1)S(1)}, u32[]{:S(2)}, u32[]{:S(2)}) collective-permute-start(bf16[256,256]{1,0:T(8,128)(2,1)S(1)} %get-tuple-element.54.refs_4_), channel_id=1, source_target_pairs={{0,192},{32,224},{64,0},{96,32},{128,64},{160,96},{192,128},{224,1... | collective-permute-start | bytes 393224 | tf_op jit(solution)/shard_map/ppermute | solution.py:21
  33.0 9.0 %collective-permute-start.7 = (bf16[272,256]{1,0:T(8,128)(2,1)S(1)}, bf16[272,256]{1,0:T(8,128)(2,1)S(1)}, u32[]{:S(2)}, u32[]{:S(2)}) collective-permute-start(bf16[272,256]{1,0:T(8,128)(2,1)S(1)} %get-tuple-element.53.refs_0_), channel_id=1, source_target_pairs={{0,192},{32,224},{64,0},{96,32},{128,64},{160,96},{192,128},{224,1... | collective-permute-start | bytes 417800 | tf_op jit(solution)/shard_map/ppermute | solution.py:21
  35.5 6.5 %collective-permute-start.8 = (bf16[272,256]{1,0:T(8,128)(2,1)S(1)}, bf16[272,256]{1,0:T(8,128)(2,1)S(1)}, u32[]{:S(2)}, u32[]{:S(2)}) collective-permute-start(bf16[272,256]{1,0:T(8,128)(2,1)S(1)} %collective-permute-done.6.refs_1_), channel_id=1, source_target_pairs={{0,64},{32,96},{64,128},{96,160},{128,192},{160,224},{192,0},{224,... | collective-permute-start | bytes 417800 | tf_op jit(solution)/shard_map/ppermute | solution.py:21
  35.5 6.5 %collective-permute-start.9 = (bf16[256,256]{1,0:T(8,128)(2,1)S(1)}, bf16[256,256]{1,0:T(8,128)(2,1)S(1)}, u32[]{:S(2)}, u32[]{:S(2)}) collective-permute-start(bf16[256,256]{1,0:T(8,128)(2,1)S(1)} %get-tuple-element.54.refs_4_), channel_id=1, source_target_pairs={{0,64},{32,96},{64,128},{96,160},{128,192},{160,224},{192,0},{224,... | collective-permute-start | bytes 393224 | tf_op jit(solution)/shard_map/ppermute | solution.py:21
  36.7 5.3 %collective-permute-start.11 = (bf16[256,256]{1,0:T(8,128)(2,1)S(1)}, bf16[256,256]{1,0:T(8,128)(2,1)S(1)}, u32[]{:S(2)}, u32[]{:S(2)}) collective-permute-start(bf16[256,256]{1,0:T(8,128)(2,1)S(1)} %collective-permute-done.10.refs_6_), channel_id=1, source_target_pairs={{0,192},{32,224},{64,0},{96,32},{128,64},{160,96},{192,128},{224,1... | collective-permute-start | bytes 393224 | tf_op jit(solution)/shard_map/ppermute | solution.py:21
  42.4 6.9 %collective-permute-start.12 = (bf16[2,256,256]{2,1,0:T(8,128)(2,1)S(1)}, bf16[2,256,256]{2,1,0:T(8,128)(2,1)S(1)}, u32[]{:S(2)}, u32[]{:S(2)}) collective-permute-start(bf16[2,256,256]{2,1,0:T(8,128)(2,1)S(1)} %get-tuple-element.56), channel_id=1, source_target_pairs={{0,32},{32,0},{64,96},{96,64},{128,160},{160,128},{192,224},{224,1... | collective-permute-start | bytes 786440 | tf_op jit(solution)/shard_map/ppermute | solution.py:351

commit v5 on v4

--- a/solution.py
+++ b/solution.py
@@ -26,8 +26,8 @@
     pairs = []
     for r in range(regions):
         for j in range(length):
-            there = j + by if j // by % 2 == parity else j - by
-            goal = (r, there) if 0 <= there < length else (r + 1 - 2 * (r % 2), j)
+            there = j + by if j // by % 2 == (parity + r) % 2 else j - by
+            goal = (r, there) if 0 <= there < length else (r ^ 2, j)
             pairs.append((r * length + j, goal[0] * length + goal[1]))
     return lax.ppermute(value, ("region", "box"), pairs)
 
@@ -71,7 +71,7 @@
 
 
 def directions():
-    odd = lax.rem(lax.axis_index("box"), 2)
+    odd = lax.rem(lax.axis_index("box") + lax.axis_index("region"), 2)
     return 1 - odd, odd
 
 

time: 50.3 us -> 51.4 us (1.022)
  waiting for transfers between devices: 11.7 us -> 15.2 us
  starting transfers between devices: 23.2 us -> 20.7 us
    ppermute x6, waiting for transfers between devices: 5.57 us -> 9.03 us  [swap(): return lax.ppermute(value, ('region', 'box'), pairs)]
    ppermute x6, starting transfers between devices: 10.7 us -> 9.16 us  [swap(): return lax.ppermute(value, ('region', 'box'), pairs)]
    ppermute x1, starting transfers between devices: 5.74 us -> 4.77 us  [local(): received = lax.ppermute(other, 'region', partners)]
  transfers between devices with their start and end apart: 13 -> 13, of which waited for: 5 -> 6; matrix products, arithmetic and copies ran while one was open for 0% -> 0% of each run, Pallas kernels for 22% -> 21%
where the time goes in v5:
time: 51.4 us; the launch traced here: 51 us
  starting transfers between devices  20.7 us (40%)
  waiting for transfers between devices  15.2 us (30%)
  Pallas kernels  14.9 us (29%)
    ppermute x6, starting transfers between devices, swap(): return lax.ppermute(value, ('region', 'box'), pairs)  9.16 us
    ppermute x6, waiting for transfers between devices, swap(): return lax.ppermute(value, ('region', 'box'), pairs)  9.03 us
    ppermute x6, starting transfers between devices, shift(): lax.ppermute(value, axis, [(i, (i + by) % length) for i in range(length)])  6.74 us
    ppermute x6, waiting for transfers between devices, shift(): lax.ppermute(value, axis, [(i, (i + by) % length) for i in range(length)])  4.98 us
    ppermute x1, starting transfers between devices, local(): received = lax.ppermute(other, 'region', partners)  4.77 us
    pallas_call x1, Pallas kernels, local(): pl.pallas_call(functools.partial(reduce_kernel, 2), in_specs=[HBM] * 4, o...  3.22 us
    pallas_call x1, Pallas kernels, self_update(): pl.pallas_call(self_kernel, grid=(places,), in_specs=[SMEM, SMEM, VMEM, b...  2.94 us
    pallas_call x1, Pallas kernels, local(): pl.pallas_call(whole_kernel, in_specs=[VMEM] * 4, out_specs=VMEM, out_sha...  2.59 us
  transfers between devices with their start and end apart: 13, of which 6 were waited for; matrix products, arithmetic and copies ran while one was open for 0% of the time, Pallas kernels for 21%

profile of v5, /device:TPU:25, one launch (start us, length us, event | category | flops | bytes accessed | tf_op | source)
XLA Modules:
  0.0 51.0 jit_solution(7512580931344495074)
XLA Ops:
  0.0 6.2 %collective-permute-start = (s32[2,256]{1,0:T(2,128)}, s32[2,256]{1,0:T(2,128)S(1)}, u32[]{:S(2)}, u32[]{:S(2)}) collective-permute-start(s32[2,256]{1,0:T(2,128)} %slots_ref), channel_id=1, source_target_pairs={{0,2},{1,3},{2,0},{3,1},{4,6},{5,7},{6,4},{7,5},{8,10},{9,11},{10,... | collective-permute-start | bytes 6152 | tf_op jit(solution)/shard_map/ppermute | solution.py:32
  6.2 1.0 %collective-permute-start.1 = (s32[2,256]{1,0:T(2,128)}, s32[2,256]{1,0:T(2,128)S(1)}, u32[]{:S(2)}, u32[]{:S(2)}) collective-permute-start(s32[2,256]{1,0:T(2,128)} %slots_ref), channel_id=1, source_target_pairs={{0,64},{1,65},{2,4},{3,5},{4,2},{5,3},{6,8},{7,9},{8,6},{9,7},{10,... | collective-permute-start | bytes 6152 | tf_op jit(solution)/shard_map/ppermute | solution.py:32
  7.2 3.2 %load_reduce.1 = (s32[2,4]{1,0:T(2,128)S(1)}, bf16[2,512,512]{2,1,0:T(8,128)(2,1)S(1)}, bf16[4,512,512]{2,1,0:T(8,128)(2,1)S(1)}, bf16[4,512,512]{2,1,0:T(8,128)(2,1)S(1)}) custom-call(s32[2,4]{1,0:T(2,128)} %table_ref.1, bf16[2,512,512]{2,1,0:T(8,128)(2,1)} %inverse_ref.2, bf16[2,4,512,512]{3,2,1,0:T(8,128)(2,1)} %refs_0_, bf16[2,4,512,512]{3,2,1,0:T(8,128)(2,1)} %refs_1_), custom_call_target="tpu_custom_call" | custom-call | tf_op jit(solution)/shard_map/load_reduce/pallas_call | solution.py:282
  10.5 1.7 %far_update.1 = (bf16[528,256]{1,0:T(8,128)(2,1)S(1)}, bf16[528,256]{1,0:T(8,128)(2,1)S(1)}) custom-call(s32[2,256]{1,0:T(2,128)S(1)} %collective-permute-done.one_ref, s32[2,256]{1,0:T(2,128)S(1)} %collective-permute-done.1.two_ref, s32[2,256]{1,0:T(2,128)S(1)} %copy-done.4, s32[2,4]{1,0:T(2,128)S(1)} %get-tuple-element.31.site_ref, ...), custom_call_target="tpu_custom_call" | custom-call | tf_op jit(solution)/shard_map/far_update/pallas_call | solution.py:297
  12.2 0.8 %collective-permute-start.2 = (bf16[528,256]{1,0:T(8,128)(2,1)S(1)}, bf16[528,256]{1,0:T(8,128)(2,1)S(1)}, u32[]{:S(2)}, u32[]{:S(2)}) collective-permute-start(bf16[528,256]{1,0:T(8,128)(2,1)S(1)} %get-tuple-element.34), channel_id=1, source_target_pairs={{0,64},{1,2},{2,1},{3,4},{4,3},{5,6},{6,5},{7,8},{8,7},{9,10},{10,... | collective-permute-start | bytes 811016 | tf_op jit(solution)/shard_map/ppermute | solution.py:32
  13.0 1.0 %collective-permute-start.3 = (bf16[528,256]{1,0:T(8,128)(2,1)S(1)}, bf16[528,256]{1,0:T(8,128)(2,1)S(1)}, u32[]{:S(2)}, u32[]{:S(2)}) collective-permute-start(bf16[528,256]{1,0:T(8,128)(2,1)S(1)} %get-tuple-element.35), channel_id=1, source_target_pairs={{0,1},{1,0},{2,3},{3,2},{4,5},{5,4},{6,7},{7,6},{8,9},{9,8},{10,11... | collective-permute-start | bytes 811016 | tf_op jit(solution)/shard_map/ppermute | solution.py:32
  13.9 2.2 %load.1 = (bf16[4,512,512]{2,1,0:T(8,128)(2,1)S(1)}, bf16[4,512,512]{2,1,0:T(8,128)(2,1)S(1)}) custom-call(bf16[2,4,512,512]{3,2,1,0:T(8,128)(2,1)} %refs_0_, bf16[2,4,512,512]{3,2,1,0:T(8,128)(2,1)} %refs_1_), custom_call_target="tpu_custom_call" | custom-call | tf_op jit(solution)/shard_map/load/pallas_call | solution.py:267
  16.2 0.0 copy-start.2
  16.2 0.0 copy-start.3
  16.2 2.6 %whole_update.1.near_ref = bf16[4,512,512]{2,1,0:T(8,128)(2,1)S(1)} custom-call(s32[2,4]{1,0:T(2,128)S(1)} %get-tuple-element.31.site_ref, bf16[2,512,512]{2,1,0:T(8,128)(2,1)S(1)} %get-tuple-element.46.inverse, bf16[4,512,512]{2,1,0:T(8,128)(2,1)S(1)} %get-tuple-element.49.right, bf16[4,512,512]{2,1,0:T(8,128)(2,1)S(1)} %get-tuple-element.50.left), custom_call_target="tpu_custom_call" | custom-call | tf_op jit(solution)/shard_map/whole_update/pallas_call | solution.py:308
  18.8 0.0 copy-start.5
  18.8 0.0 copy-start.6
  18.8 3.6 %collective-permute-done.3.two_ref = bf16[528,256]{1,0:T(8,128)(2,1)S(1)} collective-permute-done((bf16[528,256]{1,0:T(8,128)(2,1)S(1)}, bf16[528,256]{1,0:T(8,128)(2,1)S(1)}, u32[]{:S(2)}, u32[]{:S(2)}) %collective-permute-start.3) | collective-permute-done | bytes 270368 | tf_op jit(solution)/shard_map/ppermute | solution.py:32
  22.4 1.1 %near_update.1 = (bf16[2,256,256]{2,1,0:T(8,128)(2,1)S(1)}, bf16[2,256,256]{2,1,0:T(8,128)(2,1)S(1)}) custom-call(bf16[528,256]{1,0:T(8,128)(2,1)S(1)} %collective-permute-done.2.one_ref, bf16[528,256]{1,0:T(8,128)(2,1)S(1)} %collective-permute-done.3.two_ref, bf16[4,512,512]{2,1,0:T(8,128)(2,1)S(1)} %whole_update.1.near_ref), custom_call_target="tpu_custom_call" | custom-call | tf_op jit(solution)/shard_map/near_update/pallas_call | solution.py:316
  23.5 0.1 collective-permute-start.4
  23.6 0.1 collective-permute-start.5
  23.8 2.9 %self_update.1 = (f32[2,256,256]{2,1,0:T(8,128)S(1)}, f32[2,256,256]{2,1,0:T(8,128)S(1)}, bf16[16,256]{1,0:T(8,128)(2,1)S(1)}) custom-call(s32[2]{0:T(128)S(1)} %copy-done.5, s32[2]{0:T(128)S(1)} %copy-done.6, s32[2,256]{1,0:T(2,128)S(1)} %copy-done.4, bf16[2,512,512]{2,1,0:T(8,128)(2,1)S(1)} %copy-done.1, bf16[2,512,512]{2,1,0:T(8,128)(2,1)S(1)} %copy-done, ...), custom_call_target="tpu_custom_call" | custom-call | tf_op jit(solution)/shard_map/self_update/pallas_call | solution.py:254
  26.7 2.1 %collective-permute-done.4.one_ref = bf16[2,256,256]{2,1,0:T(8,128)(2,1)S(1)} collective-permute-done((bf16[2,256,256]{2,1,0:T(8,128)(2,1)S(1)}, bf16[2,256,256]{2,1,0:T(8,128)(2,1)S(1)}, u32[]{:S(2)}, u32[]{:S(2)}) %collective-permute-start.4) | collective-permute-done | bytes 262176 | tf_op jit(solution)/shard_map/ppermute | solution.py:32
  28.8 3.3 %collective-permute-done.5.two_ref = bf16[2,256,256]{2,1,0:T(8,128)(2,1)S(1)} collective-permute-done((bf16[2,256,256]{2,1,0:T(8,128)(2,1)S(1)}, bf16[2,256,256]{2,1,0:T(8,128)(2,1)S(1)}, u32[]{:S(2)}, u32[]{:S(2)}) %collective-permute-start.5) | collective-permute-done | bytes 262176 | tf_op jit(solution)/shard_map/ppermute | solution.py:32
  32.2 0.1 child.1
  32.3 1.3 %collective-permute-start.6 = (bf16[272,256]{1,0:T(8,128)(2,1)S(1)}, bf16[272,256]{1,0:T(8,128)(2,1)S(1)}, u32[]{:S(2)}, u32[]{:S(2)}) collective-permute-start(bf16[272,256]{1,0:T(8,128)(2,1)S(1)} %get-tuple-element.53.refs_0_), channel_id=1, source_target_pairs={{0,64},{32,96},{64,128},{96,160},{128,192},{160,224},{192,0},{224,... | collective-permute-start | bytes 417800 | tf_op jit(solution)/shard_map/ppermute | solution.py:21
  33.6 1.4 %collective-permute-start.10 = (bf16[256,256]{1,0:T(8,128)(2,1)S(1)}, bf16[256,256]{1,0:T(8,128)(2,1)S(1)}, u32[]{:S(2)}, u32[]{:S(2)}) collective-permute-start(bf16[256,256]{1,0:T(8,128)(2,1)S(1)} %get-tuple-element.54.refs_4_), channel_id=1, source_target_pairs={{0,192},{32,224},{64,0},{96,32},{128,64},{160,96},{192,128},{224,1... | collective-permute-start | bytes 393224 | tf_op jit(solution)/shard_map/ppermute | solution.py:21
  35.0 1.3 %collective-permute-start.7 = (bf16[272,256]{1,0:T(8,128)(2,1)S(1)}, bf16[272,256]{1,0:T(8,128)(2,1)S(1)}, u32[]{:S(2)}, u32[]{:S(2)}) collective-permute-start(bf16[272,256]{1,0:T(8,128)(2,1)S(1)} %get-tuple-element.53.refs_0_), channel_id=1, source_target_pairs={{0,192},{32,224},{64,0},{96,32},{128,64},{160,96},{192,128},{224,1... | collective-permute-start | bytes 417800 | tf_op jit(solution)/shard_map/ppermute | solution.py:21
  36.3 1.2 %collective-permute-done.6.refs_1_ = bf16[272,256]{1,0:T(8,128)(2,1)S(1)} collective-permute-done((bf16[272,256]{1,0:T(8,128)(2,1)S(1)}, bf16[272,256]{1,0:T(8,128)(2,1)S(1)}, u32[]{:S(2)}, u32[]{:S(2)}) %collective-permute-start.6) | collective-permute-done | bytes 139296 | tf_op jit(solution)/shard_map/ppermute | solution.py:21
  37.4 0.0 collective-permute-start.8
  37.5 1.2 %collective-permute-start.9 = (bf16[256,256]{1,0:T(8,128)(2,1)S(1)}, bf16[256,256]{1,0:T(8,128)(2,1)S(1)}, u32[]{:S(2)}, u32[]{:S(2)}) collective-permute-start(bf16[256,256]{1,0:T(8,128)(2,1)S(1)} %get-tuple-element.54.refs_4_), channel_id=1, source_target_pairs={{0,64},{32,96},{64,128},{96,160},{128,192},{160,224},{192,0},{224,... | collective-permute-start | bytes 393224 | tf_op jit(solution)/shard_map/ppermute | solution.py:21
  38.7 1.5 %collective-permute-start.11 = (bf16[256,256]{1,0:T(8,128)(2,1)S(1)}, bf16[256,256]{1,0:T(8,128)(2,1)S(1)}, u32[]{:S(2)}, u32[]{:S(2)}) collective-permute-start(bf16[256,256]{1,0:T(8,128)(2,1)S(1)} %collective-permute-done.10.refs_6_), channel_id=1, source_target_pairs={{0,192},{32,224},{64,0},{96,32},{128,64},{160,96},{192,128},{224,1... | collective-permute-start | bytes 393224 | tf_op jit(solution)/shard_map/ppermute | solution.py:21
  40.2 3.8 %collective-permute-done.9.refs_5_ = bf16[256,256]{1,0:T(8,128)(2,1)S(1)} collective-permute-done((bf16[256,256]{1,0:T(8,128)(2,1)S(1)}, bf16[256,256]{1,0:T(8,128)(2,1)S(1)}, u32[]{:S(2)}, u32[]{:S(2)}) %collective-permute-start.9) | collective-permute-done | bytes 131104 | tf_op jit(solution)/shard_map/ppermute | solution.py:21
  44.0 0.4 choose.1
  44.3 4.8 %collective-permute-start.12 = (bf16[2,256,256]{2,1,0:T(8,128)(2,1)S(1)}, bf16[2,256,256]{2,1,0:T(8,128)(2,1)S(1)}, u32[]{:S(2)}, u32[]{:S(2)}) collective-permute-start(bf16[2,256,256]{2,1,0:T(8,128)(2,1)S(1)} %get-tuple-element.56), channel_id=1, source_target_pairs={{0,32},{32,0},{64,96},{96,64},{128,160},{160,128},{192,224},{224,1... | collective-permute-start | bytes 786440 | tf_op jit(solution)/shard_map/ppermute | solution.py:351
  49.1 1.2 %collective-permute-done.12.b_ref = bf16[2,256,256]{2,1,0:T(8,128)(2,1)S(1)} collective-permute-done((bf16[2,256,256]{2,1,0:T(8,128)(2,1)S(1)}, bf16[2,256,256]{2,1,0:T(8,128)(2,1)S(1)}, u32[]{:S(2)}, u32[]{:S(2)}) %collective-permute-start.12) | collective-permute-done | bytes 262176 | tf_op jit(solution)/shard_map/ppermute | solution.py:351
  50.3 0.7 %join.1 = bf16[2,256,256]{2,1,0:T(8,128)(2,1)} custom-call(bf16[2,256,256]{2,1,0:T(8,128)(2,1)S(1)} %get-tuple-element.55.a_ref, bf16[2,256,256]{2,1,0:T(8,128)(2,1)S(1)} %collective-permute-done.12.b_ref), custom_call_target="tpu_custom_call" | custom-call | tf_op jit(solution)/shard_map/join/pallas_call | solution.py:352
  (17 shorter events, 0.0 us)
Async XLA Ops:
  0.0 10.4 %copy-start.4 = (s32[2,256]{1,0:T(2,128)S(1)}, s32[2,256]{1,0:T(2,128)}, u32[]{:S(2)}) copy-start(s32[2,256]{1,0:T(2,128)} %slots_ref) | copy-start | bytes 6148
  0.0 10.4 %collective-permute-start = (s32[2,256]{1,0:T(2,128)}, s32[2,256]{1,0:T(2,128)S(1)}, u32[]{:S(2)}, u32[]{:S(2)}) collective-permute-start(s32[2,256]{1,0:T(2,128)} %slots_ref), channel_id=1, source_target_pairs={{0,2},{1,3},{2,0},{3,1},{4,6},{5,7},{6,4},{7,5},{8,10},{9,11},{10,... | collective-permute-start | bytes 6152 | tf_op jit(solution)/shard_map/ppermute | solution.py:32
  6.2 4.2 %collective-permute-start.1 = (s32[2,256]{1,0:T(2,128)}, s32[2,256]{1,0:T(2,128)S(1)}, u32[]{:S(2)}, u32[]{:S(2)}) collective-permute-start(s32[2,256]{1,0:T(2,128)} %slots_ref), channel_id=1, source_target_pairs={{0,64},{1,65},{2,4},{3,5},{4,2},{5,3},{6,8},{7,9},{8,6},{9,7},{10,... | collective-permute-start | bytes 6152 | tf_op jit(solution)/shard_map/ppermute | solution.py:32
  12.2 6.7 %collective-permute-start.2 = (bf16[528,256]{1,0:T(8,128)(2,1)S(1)}, bf16[528,256]{1,0:T(8,128)(2,1)S(1)}, u32[]{:S(2)}, u32[]{:S(2)}) collective-permute-start(bf16[528,256]{1,0:T(8,128)(2,1)S(1)} %get-tuple-element.34), channel_id=1, source_target_pairs={{0,64},{1,2},{2,1},{3,4},{4,3},{5,6},{6,5},{7,8},{8,7},{9,10},{10,... | collective-permute-start | bytes 811016 | tf_op jit(solution)/shard_map/ppermute | solution.py:32
  13.0 9.5 %collective-permute-start.3 = (bf16[528,256]{1,0:T(8,128)(2,1)S(1)}, bf16[528,256]{1,0:T(8,128)(2,1)S(1)}, u32[]{:S(2)}, u32[]{:S(2)}) collective-permute-start(bf16[528,256]{1,0:T(8,128)(2,1)S(1)} %get-tuple-element.35), channel_id=1, source_target_pairs={{0,1},{1,0},{2,3},{3,2},{4,5},{5,4},{6,7},{7,6},{8,9},{9,8},{10,11... | collective-permute-start | bytes 811016 | tf_op jit(solution)/shard_map/ppermute | solution.py:32
  16.2 7.6 %copy-start.2 = (bf16[2,512,512]{2,1,0:T(8,128)(2,1)S(1)}, bf16[2,512,512]{2,1,0:T(8,128)(2,1)}, u32[]{:S(2)}) copy-start(bf16[2,512,512]{2,1,0:T(8,128)(2,1)} %by_kept_ref) | copy-start | bytes 3145732
  16.2 7.6 %copy-start.3 = (bf16[2,512,512]{2,1,0:T(8,128)(2,1)S(1)}, bf16[2,512,512]{2,1,0:T(8,128)(2,1)}, u32[]{:S(2)}) copy-start(bf16[2,512,512]{2,1,0:T(8,128)(2,1)} %by_discard_ref) | copy-start | bytes 3145732
  18.8 5.0 %copy-start = (bf16[2,512,512]{2,1,0:T(8,128)(2,1)S(1)}, bf16[2,512,512]{2,1,0:T(8,128)(2,1)}, u32[]{:S(2)}) copy-start(bf16[2,512,512]{2,1,0:T(8,128)(2,1)} %inverse_ref.2) | copy-start | bytes 3145732
  18.8 5.0 %copy-start.1 = (bf16[2,512,512]{2,1,0:T(8,128)(2,1)S(1)}, bf16[2,512,512]{2,1,0:T(8,128)(2,1)}, u32[]{:S(2)}) copy-start(bf16[2,512,512]{2,1,0:T(8,128)(2,1)} %tile_ref) | copy-start | bytes 3145732
  18.8 5.0 %copy-start.5 = (s32[2]{0:T(128)S(1)}, s32[2]{0:T(128)}, u32[]{:S(2)}) copy-start(s32[2]{0:T(128)} %length_ref) | copy-start | bytes 28
  18.8 4.9 %copy-start.6 = (s32[2]{0:T(128)S(1)}, s32[2]{0:T(128)}, u32[]{:S(2)}) copy-start(s32[2]{0:T(128)} %code_ref) | copy-start | bytes 28
  23.5 5.3 %collective-permute-start.4 = (bf16[2,256,256]{2,1,0:T(8,128)(2,1)S(1)}, bf16[2,256,256]{2,1,0:T(8,128)(2,1)S(1)}, u32[]{:S(2)}, u32[]{:S(2)}) collective-permute-start(bf16[2,256,256]{2,1,0:T(8,128)(2,1)S(1)} %get-tuple-element.51), channel_id=1, source_target_pairs={{0,64},{1,2},{2,1},{3,4},{4,3},{5,6},{6,5},{7,8},{8,7},{9,10},{10,... | collective-permute-start | bytes 786440 | tf_op jit(solution)/shard_map/ppermute | solution.py:32
  23.6 8.5 %collective-permute-start.5 = (bf16[2,256,256]{2,1,0:T(8,128)(2,1)S(1)}, bf16[2,256,256]{2,1,0:T(8,128)(2,1)S(1)}, u32[]{:S(2)}, u32[]{:S(2)}) collective-permute-start(bf16[2,256,256]{2,1,0:T(8,128)(2,1)S(1)} %get-tuple-element.52), channel_id=1, source_target_pairs={{0,1},{1,0},{2,3},{3,2},{4,5},{5,4},{6,7},{7,6},{8,9},{9,8},{10,11... | collective-permute-start | bytes 786440 | tf_op jit(solution)/shard_map/ppermute | solution.py:32
  32.3 5.2 %collective-permute-start.6 = (bf16[272,256]{1,0:T(8,128)(2,1)S(1)}, bf16[272,256]{1,0:T(8,128)(2,1)S(1)}, u32[]{:S(2)}, u32[]{:S(2)}) collective-permute-start(bf16[272,256]{1,0:T(8,128)(2,1)S(1)} %get-tuple-element.53.refs_0_), channel_id=1, source_target_pairs={{0,64},{32,96},{64,128},{96,160},{128,192},{160,224},{192,0},{224,... | collective-permute-start | bytes 417800 | tf_op jit(solution)/shard_map/ppermute | solution.py:21
  33.6 5.1 %collective-permute-start.10 = (bf16[256,256]{1,0:T(8,128)(2,1)S(1)}, bf16[256,256]{1,0:T(8,128)(2,1)S(1)}, u32[]{:S(2)}, u32[]{:S(2)}) collective-permute-start(bf16[256,256]{1,0:T(8,128)(2,1)S(1)} %get-tuple-element.54.refs_4_), channel_id=1, source_target_pairs={{0,192},{32,224},{64,0},{96,32},{128,64},{160,96},{192,128},{224,1... | collective-permute-start | bytes 393224 | tf_op jit(solution)/shard_map/ppermute | solution.py:21
  35.0 9.0 %collective-permute-start.7 = (bf16[272,256]{1,0:T(8,128)(2,1)S(1)}, bf16[272,256]{1,0:T(8,128)(2,1)S(1)}, u32[]{:S(2)}, u32[]{:S(2)}) collective-permute-start(bf16[272,256]{1,0:T(8,128)(2,1)S(1)} %get-tuple-element.53.refs_0_), channel_id=1, source_target_pairs={{0,192},{32,224},{64,0},{96,32},{128,64},{160,96},{192,128},{224,1... | collective-permute-start | bytes 417800 | tf_op jit(solution)/shard_map/ppermute | solution.py:21
  37.4 6.5 %collective-permute-start.8 = (bf16[272,256]{1,0:T(8,128)(2,1)S(1)}, bf16[272,256]{1,0:T(8,128)(2,1)S(1)}, u32[]{:S(2)}, u32[]{:S(2)}) collective-permute-start(bf16[272,256]{1,0:T(8,128)(2,1)S(1)} %collective-permute-done.6.refs_1_), channel_id=1, source_target_pairs={{0,64},{32,96},{64,128},{96,160},{128,192},{160,224},{192,0},{224,... | collective-permute-start | bytes 417800 | tf_op jit(solution)/shard_map/ppermute | solution.py:21
  37.5 6.5 %collective-permute-start.9 = (bf16[256,256]{1,0:T(8,128)(2,1)S(1)}, bf16[256,256]{1,0:T(8,128)(2,1)S(1)}, u32[]{:S(2)}, u32[]{:S(2)}) collective-permute-start(bf16[256,256]{1,0:T(8,128)(2,1)S(1)} %get-tuple-element.54.refs_4_), channel_id=1, source_target_pairs={{0,64},{32,96},{64,128},{96,160},{128,192},{160,224},{192,0},{224,... | collective-permute-start | bytes 393224 | tf_op jit(solution)/shard_map/ppermute | solution.py:21
  38.7 5.3 %collective-permute-start.11 = (bf16[256,256]{1,0:T(8,128)(2,1)S(1)}, bf16[256,256]{1,0:T(8,128)(2,1)S(1)}, u32[]{:S(2)}, u32[]{:S(2)}) collective-permute-start(bf16[256,256]{1,0:T(8,128)(2,1)S(1)} %collective-permute-done.10.refs_6_), channel_id=1, source_target_pairs={{0,192},{32,224},{64,0},{96,32},{128,64},{160,96},{192,128},{224,1... | collective-permute-start | bytes 393224 | tf_op jit(solution)/shard_map/ppermute | solution.py:21
  44.3 5.9 %collective-permute-start.12 = (bf16[2,256,256]{2,1,0:T(8,128)(2,1)S(1)}, bf16[2,256,256]{2,1,0:T(8,128)(2,1)S(1)}, u32[]{:S(2)}, u32[]{:S(2)}) collective-permute-start(bf16[2,256,256]{2,1,0:T(8,128)(2,1)S(1)} %get-tuple-element.56), channel_id=1, source_target_pairs={{0,32},{32,0},{64,96},{96,64},{128,160},{160,128},{192,224},{224,1... | collective-permute-start | bytes 786440 | tf_op jit(solution)/shard_map/ppermute | solution.py:351
